TPU v7x, 32 devices: a whole 2x2x4 slice. The times are simulated.
32 devices in a mesh: seq: 16 (over z, y, x), chan: 2 (over core).
Axes of the slice: x: 2, y: 2, z: 4, core: 2. Of those that a mesh axis runs over, the one named last changes fastest.
Arguments:
- query_in: bfloat16 [2048, 2048], P('chan', 'seq'), may hold values from -6 to 6
- key_in: bfloat16 [2048, 2048], P('chan', 'seq'), may hold values from -6 to 6
- value_in: bfloat16 [2048, 2048], P('chan', 'seq'), may hold values from -6 to 6
- short_weight: float32 [3, 7, 2048], P(None, None, 'chan'), may hold values from -2 to 2
- residue: float32 [2048, 16], P(('chan', 'seq')), may hold values from -1.5 to 1.5
- log_rate: float32 [2048, 16], P(('chan', 'seq')), may hold values from -13 to -3.2
- grad_out: bfloat16 [2048, 2048], P('chan', 'seq'), may hold values from -6 to 6
Outputs:
- output: bfloat16 [2048, 2048], P('chan', 'seq')
- grad_query: bfloat16 [2048, 2048], P('chan', 'seq')
- grad_key: bfloat16 [2048, 2048], P('chan', 'seq')
- grad_value: bfloat16 [2048, 2048], P('chan', 'seq')
- grad_short: float32 [3, 7, 2048], P(None, None, 'chan')
- grad_residue: float32 [2048, 16], P(('chan', 'seq'))
- grad_log_rate: float32 [2048, 16], P(('chan', 'seq'))
All inputs are finite; a program needn't handle non-finite values.
Results may differ from a plain program's by a relative error of at most 0.008.
Values may be sent and summed in bfloat16 or wider, within the bound.
A program may use at most 64 MiB of HBM per device.

v0:
```python
import functools
import math

import jax
import jax.numpy as jnp
from jax import lax
from jax.experimental import pallas as pl
from jax.experimental.pallas import tpu as pltpu
from jax.sharding import PartitionSpec as P


def shifted(shard, axis, by):
    count = lax.axis_size(axis)
    pairs = [(i, i + by) for i in range(count) if 0 <= i + by < count]
    return lax.ppermute(shard, axis, pairs)


def dft_table(length, sign):
    counter = jnp.arange(length, dtype=jnp.int32)
    product = counter[:, None] * counter[None, :] % length
    angle = product.astype(jnp.float32) * (sign * 2.0 * math.pi / length)
    return (jnp.cos(angle), jnp.sin(angle))


def complex_dot(real_part, imag_part, table_real, table_imag):
    highest = lax.Precision.HIGHEST
    out_real = jnp.matmul(real_part, table_real, precision=highest) - jnp.matmul(
        imag_part, table_imag, precision=highest
    )
    out_imag = jnp.matmul(real_part, table_imag, precision=highest) + jnp.matmul(
        imag_part, table_real, precision=highest
    )
    return (out_real, out_imag)


def transform(real_part, imag_part, sign):
    length = real_part.shape[-1]
    if length <= 256 or length % 128 != 0:
        table_real, table_imag = dft_table(length, sign)
        return complex_dot(real_part, imag_part, table_real, table_imag)
    outer = 128
    inner = length // outer
    leading = real_part.shape[:-1]
    split_real = jnp.swapaxes(real_part.reshape(leading + (inner, outer)), -1, -2)
    split_imag = jnp.swapaxes(imag_part.reshape(leading + (inner, outer)), -1, -2)
    part_real, part_imag = transform(split_real, split_imag, sign)
    first_index = jnp.arange(outer, dtype=jnp.int32)[:, None]
    second_index = jnp.arange(inner, dtype=jnp.int32)[None, :]
    angle = (first_index * second_index % length).astype(jnp.float32) * (
        sign * 2.0 * math.pi / length
    )
    twist_real = jnp.cos(angle)
    twist_imag = jnp.sin(angle)
    turned_real = part_real * twist_real - part_imag * twist_imag
    turned_imag = part_real * twist_imag + part_imag * twist_real
    table_real, table_imag = dft_table(outer, sign)
    highest = lax.Precision.HIGHEST
    out_real = jnp.einsum(
        "...nk,nl->...lk", turned_real, table_real, precision=highest
    ) - jnp.einsum("...nk,nl->...lk", turned_imag, table_imag, precision=highest)
    out_imag = jnp.einsum(
        "...nk,nl->...lk", turned_real, table_imag, precision=highest
    ) + jnp.einsum("...nk,nl->...lk", turned_imag, table_real, precision=highest)
    return (out_real.reshape(leading + (length,)), out_imag.reshape(leading + (length,)))


def spectrum(signal):
    length = signal.shape[1]
    padded = jnp.pad(signal.astype(jnp.float32), ((0, 0), (0, length)))
    return transform(padded, jnp.zeros_like(padded), -1.0)


def mirrored(values):
    return jnp.roll(jnp.flip(values, -1), 1, -1)


def paired_spectra(first, second):
    length = first.shape[1]
    first_pad = jnp.pad(first, ((0, 0), (0, length)))
    second_pad = jnp.pad(second.astype(jnp.float32), ((0, 0), (0, length)))
    joint_real, joint_imag = transform(first_pad, second_pad, -1.0)
    mirror_real = mirrored(joint_real)
    mirror_imag = mirrored(joint_imag)
    first_spec = (0.5 * (joint_real + mirror_real), 0.5 * (joint_imag - mirror_imag))
    second_spec = (0.5 * (joint_imag + mirror_imag), -0.5 * (joint_real - mirror_real))
    return (first_spec, second_spec)


def to_time(spec_pair, length):
    real_part, imag_part = spec_pair
    back_real, back_imag = transform(real_part, imag_part, 1.0)
    return back_real[:, :length] / real_part.shape[-1]


def paired_time(first_spec, second_spec, length):
    joint_real = first_spec[0] - second_spec[1]
    joint_imag = first_spec[1] + second_spec[0]
    back_real, back_imag = transform(joint_real, joint_imag, 1.0)
    total_len = joint_real.shape[-1]
    return (back_real[:, :length] / total_len, back_imag[:, :length] / total_len)


def spectral_product(first, second, conjugate):
    first_real, first_imag = first
    second_real, second_imag = second
    if conjugate:
        second_imag = -second_imag
    return (
        first_real * second_real - first_imag * second_imag,
        first_real * second_imag + first_imag * second_real,
    )


def modal_filter(residue, log_rate, length):
    decay_rate = jnp.exp(log_rate)
    offsets = jnp.arange(length).astype(jnp.float32)
    filt = jnp.zeros((residue.shape[0], length), jnp.float32)
    for mode_index in range(residue.shape[1]):
        factor = residue[:, mode_index] * jnp.sqrt(2.0 * decay_rate[:, mode_index])
        filt = filt + factor[:, None] * jnp.exp(-decay_rate[:, mode_index][:, None] * offsets)
    return filt


def modal_grads(filt_grad, residue, log_rate):
    decay_rate = jnp.exp(log_rate)
    offsets = jnp.arange(filt_grad.shape[1]).astype(jnp.float32)
    res_terms = []
    log_terms = []
    for mode_index in range(residue.shape[1]):
        rate_col = decay_rate[:, mode_index][:, None]
        basis = jnp.sqrt(2.0 * rate_col) * jnp.exp(-rate_col * offsets)
        weighted = filt_grad * basis
        res_terms.append(jnp.sum(weighted, axis=1))
        log_terms.append(
            residue[:, mode_index] * jnp.sum(weighted * (0.5 - rate_col * offsets), axis=1)
        )
    return (jnp.stack(res_terms, axis=1), jnp.stack(log_terms, axis=1))


def apply_taps(widened, taps, tok_rows):
    total = jnp.zeros((widened.shape[0], tok_rows), jnp.float32)
    for offset in range(7):
        total = total + taps[offset][:, None] * widened[:, 6 - offset : 6 - offset + tok_rows]
    return total


def taps_back(gradient, following, taps):
    tok_rows = gradient.shape[1]
    widened = jnp.concatenate([gradient, following], axis=1)
    total = jnp.zeros_like(gradient)
    for offset in range(7):
        total = total + taps[offset][:, None] * widened[:, offset : offset + tok_rows]
    return total


def taps_gradient(gradient, widened):
    tok_rows = gradient.shape[1]
    rows_out = [
        jnp.sum(gradient * widened[:, 6 - offset : 6 - offset + tok_rows], axis=1)
        for offset in range(7)
    ]
    return jnp.stack(rows_out, axis=0)


def to_channels(stream):
    return lax.all_to_all(stream, "seq", split_axis=0, concat_axis=1, tiled=True)


def to_tokens(stream):
    return lax.all_to_all(stream, "seq", split_axis=1, concat_axis=0, tiled=True)


def local_fft(query_in, key_in, value_in, short_weight, residue, log_rate, grad_out):
    tok_rows = query_in.shape[1]
    length = tok_rows * lax.axis_size("seq")
    scale = 1.0 / math.sqrt(length)
    tails = shifted((query_in[:, -6:], key_in[:, -6:], value_in[:, -6:]), "seq", 1)
    query_wide = jnp.concatenate([tails[0], query_in], axis=1).astype(jnp.float32)
    key_wide = jnp.concatenate([tails[1], key_in], axis=1).astype(jnp.float32)
    value_wide = jnp.concatenate([tails[2], value_in], axis=1).astype(jnp.float32)
    query_hat = apply_taps(query_wide, short_weight[0], tok_rows)
    key_hat = apply_taps(key_wide, short_weight[1], tok_rows)
    value_hat = apply_taps(value_wide, short_weight[2], tok_rows)
    mixed = (key_hat * value_hat).astype(jnp.bfloat16)
    grad_up = grad_out.astype(jnp.float32)
    grad_mixed = (grad_up * query_hat).astype(jnp.bfloat16)
    mixed_cols = to_channels(mixed)
    filt = modal_filter(residue, log_rate, length)
    spec_filter, spec_mixed = paired_spectra(filt, mixed_cols)
    long_out = to_time(spectral_product(spec_mixed, spec_filter, False), length).astype(
        jnp.bfloat16
    )
    conv_out = to_tokens(long_out)
    grad_cols = to_channels(grad_mixed)
    spec_grad = spectrum(grad_cols)
    long_grad, filt_grad = paired_time(
        spectral_product(spec_grad, spec_filter, True),
        spectral_product(spec_grad, spec_mixed, True),
        length,
    )
    conv_grad = to_tokens(long_grad.astype(jnp.bfloat16))
    grad_res, grad_log = modal_grads(filt_grad, residue, log_rate)
    conv_wide = conv_out.astype(jnp.float32)
    conv_grad_wide = conv_grad.astype(jnp.float32)
    output = (query_hat * conv_wide).astype(jnp.bfloat16)
    grad_q = grad_up * conv_wide
    grad_k = conv_grad_wide * value_hat
    grad_v = conv_grad_wide * key_hat
    heads = shifted((grad_q[:, :6], grad_k[:, :6], grad_v[:, :6]), "seq", -1)
    grad_query = taps_back(grad_q, heads[0], short_weight[0]).astype(jnp.bfloat16)
    grad_key = taps_back(grad_k, heads[1], short_weight[1]).astype(jnp.bfloat16)
    grad_value = taps_back(grad_v, heads[2], short_weight[2]).astype(jnp.bfloat16)
    local_terms = jnp.stack(
        [
            taps_gradient(grad_q, query_wide),
            taps_gradient(grad_k, key_wide),
            taps_gradient(grad_v, value_wide),
        ],
        axis=0,
    )
    grad_short = lax.psum(local_terms, "seq") * scale
    return (
        output,
        grad_query,
        grad_key,
        grad_value,
        grad_short,
        grad_res * scale,
        grad_log * scale,
    )


SUB = 8
LANE = 128
HALO = 6
TAPS = 7
GROUP = 8
MESH = pl.DeviceIdType.MESH


def slab(index):
    return pl.ds(pl.multiple_of(index * SUB, SUB), SUB)


def layer_kernel(
    n, modes, tokens, scale,
    query_ref, key_ref, value_ref, grad_ref, weight_ref, param_ref,
    out_ref, gq_ref, gk_ref, gv_ref, short_ref, modal_ref,
    streams, hats, mixed, gmixed, conv, conv_back, prod, cots,
    params, decay, gain, rate,
    fwd_send, fwd_recv, bwd_send, bwd_recv, acc_send, acc_recv,
    carry_send, carry_recv, modal_send, modal_recv,
    short_send, short_recv, total_send, total_recv,
    send_sem, recv_sem, halo_send, halo_recv,
):
    me = lax.axis_index("seq")
    extent = tokens + HALO
    f32 = jnp.float32
    zero = jnp.zeros((SUB, LANE), f32)

    def rounded(value):
        return value.astype(jnp.bfloat16).astype(f32)

    def exchange(phase, k, source, target):
        peer = lax.rem(me + k, n)
        return pltpu.make_async_remote_copy(
            src_ref=source(peer),
            dst_ref=target(me),
            send_sem=send_sem.at[phase, k],
            recv_sem=recv_sem.at[phase, k],
            device_id={"seq": peer},
            device_id_type=MESH,
        )

    def start_all(phase, source, target):
        def step(k, carry):
            exchange(phase, k, source, target).start()
            return carry

        lax.fori_loop(1, n, step, 0)

    def wait_all(phase, source, target):
        def step(k, carry):
            exchange(phase, k, source, target).wait()
            return carry

        lax.fori_loop(1, n, step, 0)

    barrier = pltpu.get_barrier_semaphore()

    def greet(k, carry):
        pl.semaphore_signal(
            barrier, inc=1, device_id={"seq": lax.rem(me + k, n)}, device_id_type=MESH
        )
        return carry

    lax.fori_loop(1, n, greet, 0)

    ins = (query_ref, key_ref, value_ref, grad_ref)
    for s in range(4):
        for b in range(SUB):
            block = ins[s][b * LANE : (b + 1) * LANE, :].astype(f32)
            streams[s, pl.ds(HALO * SUB + b, tokens, stride=SUB), :] = block.T

    pl.semaphore_wait(barrier, n - 1)

    edge = HALO * SUB
    last = tokens * SUB
    to_right = lambda: pltpu.make_async_remote_copy(
        src_ref=streams.at[pl.ds(0, 3), pl.ds(last, edge)],
        dst_ref=streams.at[pl.ds(0, 3), pl.ds(0, edge)],
        send_sem=halo_send.at[0],
        recv_sem=halo_recv.at[0],
        device_id={"seq": lax.rem(me + 1, n)},
        device_id_type=MESH,
    )
    to_left = lambda: pltpu.make_async_remote_copy(
        src_ref=streams.at[:, pl.ds(edge, edge)],
        dst_ref=streams.at[:, pl.ds(edge + last, edge)],
        send_sem=halo_send.at[1],
        recv_sem=halo_recv.at[1],
        device_id={"seq": lax.rem(me + n - 1, n)},
        device_id_type=MESH,
    )

    @pl.when(me < n - 1)
    def _():
        to_right().start()

    @pl.when(me > 0)
    def _():
        to_left().start()

    @pl.when(me == 0)
    def _():
        streams[0:3, 0:edge, :] = jnp.zeros((3, edge, LANE), f32)

    @pl.when(me == n - 1)
    def _():
        streams[:, edge + last : 2 * edge + last, :] = jnp.zeros((4, edge, LANE), f32)

    own_rows = pl.ds(pl.multiple_of(me * modes, modes), modes)
    par_src = lambda peer: param_ref
    par_dst = lambda owner: params.at[pl.ds(pl.multiple_of(owner * modes, modes), modes)]
    start_all(0, par_src, par_dst)
    params[own_rows, :] = param_ref[...]

    taps = [[weight_ref[s * TAPS + j] for j in range(TAPS)] for s in range(3)]

    def filter_token(t):
        vals = []
        for s in range(3):
            total = taps[s][0] * streams[s, slab(t + HALO), :]
            for j in range(1, TAPS):
                total = total + taps[s][j] * streams[s, slab(t + HALO - j), :]
            hats[s, slab(t), :] = total
            vals.append(total)
        mixed[slab(t), :] = rounded(vals[1] * vals[2])
        gmixed[slab(t), :] = rounded(vals[0] * streams[3, slab(t + HALO), :])

    def token_loop(lo, hi, unroll, fn):
        def step(i, carry):
            for u in range(unroll):
                fn(lo + i * unroll + u)
            return carry

        lax.fori_loop(0, (hi - lo) // unroll, step, 0)

    token_loop(HALO, tokens, 2, filter_token)

    @pl.when(me > 0)
    def _():
        to_left().wait_send()
        to_right().wait_recv()

    @pl.when(me < n - 1)
    def _():
        to_right().wait_send()
        to_left().wait_recv()

    token_loop(0, HALO, 2, filter_token)
    token_loop(tokens, extent, 2, filter_token)

    wait_all(0, par_src, par_dst)
    low_half = lax.broadcasted_iota(jnp.int32, (SUB, LANE), 1) < LANE // 2
    for m in range(modes):
        even = params[pl.ds(m, SUB, stride=2 * modes), :]
        odd = params[pl.ds(modes + m, SUB, stride=2 * modes), :]
        log_rate = jnp.where(low_half, even, pltpu.roll(odd, LANE // 2, 1))
        residue = jnp.where(low_half, pltpu.roll(even, LANE // 2, 1), odd)
        r = jnp.exp(log_rate)
        rate[slab(m), :] = r
        decay[slab(m), :] = jnp.exp(-r)
        gain[slab(m), :] = residue * jnp.sqrt(2.0 * r)

    UN = 4
    for first in range(0, modes, GROUP):
        group = range(first, first + GROUP)

        def fwd_step(i, carry, first=first, group=group):
            x, y, ax, ay = [list(c) for c in carry]
            for u in range(UN):
                t = i * UN + u
                value = mixed[slab(t), :]
                cot = gmixed[slab(t), :]
                total = conv[slab(t), :] if first else zero
                for p, m in enumerate(group):
                    a = decay[m * SUB : (m + 1) * SUB, :]
                    y[p] = a * (y[p] + x[p])
                    x[p] = a * x[p] + value
                    total = total + gain[m * SUB : (m + 1) * SUB, :] * x[p]
                    ax[p] = ax[p] + cot * x[p]
                    ay[p] = ay[p] + cot * y[p]
                conv[slab(t), :] = total
            return tuple(tuple(c) for c in (x, y, ax, ay))

        zeros = tuple(zero for _ in group)
        x, y, ax, ay = lax.fori_loop(0, tokens // UN, fwd_step, (zeros,) * 4)
        for p, m in enumerate(group):
            fwd_send[m, 0:SUB, :] = x[p]
            fwd_send[m, SUB : 2 * SUB, :] = y[p]
            acc_send[m, 0:SUB, :] = ax[p]
            acc_send[m, SUB : 2 * SUB, :] = ay[p]
        x = list(x)
        for t in range(tokens, extent):
            value = mixed[t * SUB : (t + 1) * SUB, :]
            total = conv[t * SUB : (t + 1) * SUB, :] if first else zero
            for p, m in enumerate(group):
                x[p] = decay[m * SUB : (m + 1) * SUB, :] * x[p] + value
                total = total + gain[m * SUB : (m + 1) * SUB, :] * x[p]
            conv[t * SUB : (t + 1) * SUB, :] = total

    fwd_src = lambda peer: fwd_send.at[peer]
    fwd_dst = lambda owner: fwd_recv.at[owner]
    start_all(1, fwd_src, fwd_dst)

    for first in range(0, modes, GROUP):
        group = range(first, first + GROUP)

        def bwd_step(i, carry, first=first, group=group):
            z, w = [list(c) for c in carry]
            for u in range(UN):
                t = tokens - 1 - (i * UN + u)
                cot = gmixed[slab(t), :]
                total = conv_back[slab(t), :] if first else zero
                for p, m in enumerate(group):
                    a = decay[m * SUB : (m + 1) * SUB, :]
                    z[p] = a * z[p] + cot
                    w[p] = a * w[p] + z[p]
                    total = total + gain[m * SUB : (m + 1) * SUB, :] * z[p]
                conv_back[slab(t), :] = total
            return tuple(tuple(c) for c in (z, w))

        zeros = tuple(zero for _ in group)
        z, w = lax.fori_loop(0, tokens // UN, bwd_step, (zeros,) * 2)
        for p, m in enumerate(group):
            bwd_send[m, 0:SUB, :] = z[p]
            bwd_send[m, SUB : 2 * SUB, :] = w[p]

    bwd_src = lambda peer: bwd_send.at[peer]
    bwd_dst = lambda owner: bwd_recv.at[owner]
    start_all(2, bwd_src, bwd_dst)
    acc_src = lambda peer: acc_send.at[peer]
    acc_dst = lambda owner: acc_recv.at[owner]
    start_all(3, acc_src, acc_dst)

    fwd_recv[me] = fwd_send[me]
    bwd_recv[me] = bwd_send[me]
    acc_recv[me] = acc_send[me]
    my_rate = rate[slab(me), :]
    my_decay = decay[slab(me), :]
    my_gain = gain[slab(me), :]
    whole = jnp.exp(-float(tokens) * my_rate)
    wait_all(1, fwd_src, fwd_dst)

    def scan_fwd(d, h):
        carry_send[d, 0:SUB, :] = h
        return whole * h + fwd_recv[d, 0:SUB, :]

    lax.fori_loop(0, n, scan_fwd, zero)
    wait_all(2, bwd_src, bwd_dst)

    def scan_bwd(i, z):
        d = n - 1 - i
        carry_send[d, SUB : 2 * SUB, :] = z
        return whole * z + bwd_recv[d, 0:SUB, :]

    lax.fori_loop(0, n, scan_bwd, zero)
    carry_src = lambda peer: carry_send.at[peer]
    carry_dst = lambda owner: carry_recv.at[owner]
    start_all(4, carry_src, carry_dst)
    carry_recv[me] = carry_send[me]

    wait_all(3, acc_src, acc_dst)

    def scan_acc(d, carry):
        hy, acc_x, acc_y = carry
        h = carry_send[d, 0:SUB, :]
        z0 = my_decay * bwd_recv[d, 0:SUB, :]
        z1 = my_decay * bwd_recv[d, SUB : 2 * SUB, :]
        acc_x = acc_x + (acc_recv[d, 0:SUB, :] + h * z0)
        acc_y = acc_y + (acc_recv[d, SUB : 2 * SUB, :] + h * z1 + hy * z0)
        hy = whole * (hy + float(tokens) * h) + fwd_recv[d, SUB : 2 * SUB, :]
        return hy, acc_x, acc_y

    _, acc_x, acc_y = lax.fori_loop(0, n, scan_acc, (zero, zero, zero))
    modal_send[0:SUB, :] = acc_x * jnp.sqrt(2.0 * my_rate) * scale
    modal_send[SUB : 2 * SUB, :] = my_gain * (0.5 * acc_x - my_rate * acc_y) * scale
    modal_src = lambda peer: modal_send
    modal_dst = lambda owner: modal_recv.at[owner]
    start_all(5, modal_src, modal_dst)
    modal_recv[me] = modal_send[...]

    wait_all(4, carry_src, carry_dst)

    def finish_fwd(t, c):
        c = [decay[m * SUB : (m + 1) * SUB, :] * c[m] for m in range(modes)]
        parts = c
        while len(parts) > 1:
            parts = [parts[i] + parts[i + 1] for i in range(0, len(parts), 2)]
        total = rounded(conv[slab(t), :] + parts[0])
        prod[slab(t), :] = hats[0, slab(t), :] * total
        cots[0, slab(t), :] = streams[3, slab(t + HALO), :] * total
        return c

    def fwd_two(i, c):
        c = list(c)
        for u in range(2):
            c = finish_fwd(i * 2 + u, c)
        return tuple(c)

    start = tuple(
        gain[m * SUB : (m + 1) * SUB, :] * carry_recv[m, 0:SUB, :] for m in range(modes)
    )
    lax.fori_loop(0, extent // 2, fwd_two, start)

    def store_back(t, total):
        total = rounded(total)
        cots[1, slab(t), :] = hats[2, slab(t), :] * total
        cots[2, slab(t), :] = hats[1, slab(t), :] * total

    def bwd_two(i, c):
        c = list(c)
        for u in range(2):
            t = tokens - 1 - (i * 2 + u)
            c = [decay[m * SUB : (m + 1) * SUB, :] * c[m] for m in range(modes)]
            parts = c
            while len(parts) > 1:
                parts = [parts[k] + parts[k + 1] for k in range(0, len(parts), 2)]
            store_back(t, conv_back[slab(t), :] + parts[0])
        return tuple(c)

    start = tuple(
        gain[m * SUB : (m + 1) * SUB, :] * carry_recv[m, SUB : 2 * SUB, :]
        for m in range(modes)
    )
    lax.fori_loop(0, tokens // 2, bwd_two, start)

    for h in range(HALO):
        conv_back[(tokens + h) * SUB : (tokens + h + 1) * SUB, :] = zero
    for m in range(modes):
        grow = jnp.exp(rate[m * SUB : (m + 1) * SUB, :])
        z = carry_recv[m, SUB : 2 * SUB, :]
        weight = gain[m * SUB : (m + 1) * SUB, :]
        for h in range(HALO):
            rows = slice((tokens + h) * SUB, (tokens + h + 1) * SUB)
            conv_back[rows, :] = conv_back[rows, :] + weight * z
            z = grow * (z - gmixed[rows, :])
    for h in range(HALO):
        t = tokens + h
        store_back(t, conv_back[t * SUB : (t + 1) * SUB, :])

    def short_step(i, accs):
        accs = list(accs)
        for u in range(2):
            t = i * 2 + u
            for s in range(3):
                cot = cots[s, slab(t), :]
                for j in range(TAPS):
                    at = s * TAPS + j
                    accs[at] = accs[at] + cot * streams[s, slab(t + HALO - j), :]
        return tuple(accs)

    accs = lax.fori_loop(0, tokens // 2, short_step, (zero,) * (3 * TAPS))
    for row in range(2 * n):
        short_send[row // 2, (row % 2) * SUB : (row % 2 + 1) * SUB, :] = (
            accs[row] if row < 3 * TAPS else zero
        )
    short_src = lambda peer: short_send.at[peer]
    short_dst = lambda owner: short_recv.at[owner]
    start_all(6, short_src, short_dst)
    short_recv[me] = short_send[me]

    def taps_step(t):
        for s in range(3):
            total = taps[s][0] * cots[s, slab(t), :]
            for j in range(1, TAPS):
                total = total + taps[s][j] * cots[s, slab(t + j), :]
            hats[s, slab(t), :] = total

    token_loop(0, tokens, 2, taps_step)

    wait_all(6, short_src, short_dst)
    total = short_recv[0]
    for d in range(1, n):
        total = total + short_recv[d]
    total_send[...] = total * scale
    total_src = lambda peer: total_send
    total_dst = lambda owner: total_recv.at[owner]
    start_all(7, total_src, total_dst)
    total_recv[me] = total_send[...]

    for b in range(SUB):
        rows = slice(b * LANE, (b + 1) * LANE)
        out_ref[rows, :] = prod[pl.ds(b, tokens, stride=SUB), :].T.astype(jnp.bfloat16)
    for s, ref in enumerate((gq_ref, gk_ref, gv_ref)):
        for b in range(SUB):
            rows = slice(b * LANE, (b + 1) * LANE)
            ref[rows, :] = hats[s, pl.ds(b, tokens, stride=SUB), :].T.astype(jnp.bfloat16)

    wait_all(5, modal_src, modal_dst)
    modal_ref[...] = modal_recv[...]
    wait_all(7, total_src, total_dst)
    short_ref[...] = total_recv[...]


def local(query_in, key_in, value_in, short_weight, residue, log_rate, grad_out):
    n = lax.axis_size("seq")
    width, tokens = query_in.shape
    own, modes = residue.shape
    fits = width == SUB * LANE and tokens == LANE and modes == n == 2 * SUB
    if not (fits and own == LANE // 2):
        return local_fft(
            query_in, key_in, value_in, short_weight, residue, log_rate, grad_out
        )
    scale = 1.0 / math.sqrt(tokens * n)
    f32 = jnp.float32
    rows = (tokens + HALO) * SUB
    weight = short_weight.reshape(3 * TAPS, SUB, LANE)
    param = jnp.concatenate([log_rate.T, residue.T], axis=1)
    vmem = pl.BlockSpec(memory_space=pltpu.VMEM)
    stage = pltpu.VMEM((n, 2 * SUB, LANE), f32)
    flat = pltpu.VMEM((rows, LANE), f32)
    small = pltpu.VMEM((modes * SUB, LANE), f32)
    shape = jax.ShapeDtypeStruct((width, tokens), jnp.bfloat16)
    table = jax.ShapeDtypeStruct((n, 2 * SUB, LANE), f32)
    out, gq, gk, gv, short, modal = pl.pallas_call(
        functools.partial(layer_kernel, n, modes, tokens, scale),
        out_shape=(shape, shape, shape, shape, table, table),
        in_specs=[vmem] * 6,
        out_specs=(vmem,) * 6,
        scratch_shapes=[
            pltpu.VMEM((4, rows + HALO * SUB, LANE), f32),
            pltpu.VMEM((3, rows, LANE), f32),
            flat, flat, flat, flat, flat,
            pltpu.VMEM((3, rows, LANE), f32),
            pltpu.VMEM((n * modes, LANE), f32),
            small, small, small,
            stage, stage, stage, stage, stage, stage,
            stage, stage, pltpu.VMEM((2 * SUB, LANE), f32), stage,
            stage, stage, pltpu.VMEM((2 * SUB, LANE), f32), stage,
            pltpu.SemaphoreType.DMA((8, n)),
            pltpu.SemaphoreType.DMA((8, n)),
            pltpu.SemaphoreType.DMA((2,)),
            pltpu.SemaphoreType.DMA((2,)),
        ],
        compiler_params=pltpu.CompilerParams(
            collective_id=0, has_side_effects=True, vmem_limit_bytes=40 * 2**20
        ),
    )(query_in, key_in, value_in, grad_out, weight, param)
    short = short.reshape(2 * n, width)[: 3 * TAPS].reshape(3, TAPS, width)
    modal = modal.reshape(modes, 2, width)
    mine = lax.dynamic_slice_in_dim(modal, lax.axis_index("seq") * own, own, 2)
    return (out, gq, gk, gv, short, mine[:, 0].T, mine[:, 1].T)


def solution(mesh):
    return jax.shard_map(
        local,
        mesh=mesh,
        in_specs=(
            P("chan", "seq"),
            P("chan", "seq"),
            P("chan", "seq"),
            P(None, None, "chan"),
            P(("chan", "seq"), None),
            P(("chan", "seq"), None),
            P("chan", "seq"),
        ),
        out_specs=(
            P("chan", "seq"),
            P("chan", "seq"),
            P("chan", "seq"),
            P("chan", "seq"),
            P(None, None, "chan"),
            P(("chan", "seq"), None),
            P(("chan", "seq"), None),
        ),
        check_vma=False,
    )
```

profile of v0, /device:TPU:0, one launch (start us, length us, event | category | flops | bytes accessed | tf_op | source)
XLA Modules:
  0.0 58.1 jit_solution(12297296067498536857)
XLA Ops:
  0.6 0.0 copy-start.4
  0.6 0.0 copy-start.5
  0.7 0.9 %reshape.26.weight_ref = f32[21,8,128]{2,1,0:T(8,128)S(1)} reshape(f32[3,7,1024]{2,1,0:T(8,128)} %param.10) | data formatting | bytes 172032 | tf_op jit(solution)/shard_map/reshape | solution.py:639
  1.6 0.0 copy-done.4
  1.6 0.0 copy-done.5
  1.6 0.1 pad_maximum_fusion.param_ref
  1.7 0.0 copy-start
  1.7 0.9 %copy-done = bf16[1024,128]{1,0:T(8,128)(2,1)S(1)} copy-done((bf16[1024,128]{1,0:T(8,128)(2,1)S(1)}, bf16[1024,128]{1,0:T(8,128)(2,1)}, u32[]{:S(2)}) %copy-start) | copy-done | bytes 262168
  2.6 0.0 copy-start.1
  2.6 0.9 %copy-done.1 = bf16[1024,128]{1,0:T(8,128)(2,1)S(1)} copy-done((bf16[1024,128]{1,0:T(8,128)(2,1)S(1)}, bf16[1024,128]{1,0:T(8,128)(2,1)}, u32[]{:S(2)}) %copy-start.1) | copy-done | bytes 262168
  3.6 0.0 copy-start.2
  3.6 0.9 %copy-done.2 = bf16[1024,128]{1,0:T(8,128)(2,1)S(1)} copy-done((bf16[1024,128]{1,0:T(8,128)(2,1)S(1)}, bf16[1024,128]{1,0:T(8,128)(2,1)}, u32[]{:S(2)}) %copy-start.2) | copy-done | bytes 262168
  4.5 0.0 copy-start.3
  4.5 0.9 %copy-done.3 = bf16[1024,128]{1,0:T(8,128)(2,1)S(1)} copy-done((bf16[1024,128]{1,0:T(8,128)(2,1)S(1)}, bf16[1024,128]{1,0:T(8,128)(2,1)}, u32[]{:S(2)}) %copy-start.3) | copy-done | bytes 262168
  5.5 48.3 %shard_map.126 = (bf16[1024,128]{1,0:T(8,128)(2,1)S(1)}, bf16[1024,128]{1,0:T(8,128)(2,1)S(1)}, bf16[1024,128]{1,0:T(8,128)(2,1)S(1)}, bf16[1024,128]{1,0:T(8,12...) custom-call(bf16[1024,128]{1,0:T(8,128)(2,1)S(1)} %copy-done, bf16[1024,128]{1,0:T(8,128)(2,1)S(1)} %copy-done.1, ...), custom_call_target="tpu_custom_call" | custom-call | tf_op jit(solution)/shard_map/pallas_call | solution.py:647
  53.8 0.1 reshape.29
  53.9 0.7 %constant_dynamic-slice_fusion.1 = (f32[16,1,64]{2,1,0:T(1,128)}, f32[16,1,64]{2,1,0:T(1,128)}) fusion(f32[16,2,1024]{2,1,0:T(2,128)S(1)} %reshape.29, s32[]{:T(128)S(6)} %add.4, s32[]{:T(128)S(6)} %select_n.3), kind=kLoop, calls=%fused_computation.2 | loop fusion | bytes 16392 | tf_op jit(solution)/shard_map/slice | solution.py:674
  54.7 0.7 %reshape.28 = f32[3,7,1024]{2,1,0:T(8,128)} reshape(f32[21,1024]{1,0:T(8,128)S(1)} %slice.12) | data formatting | bytes 172032 | tf_op jit(solution)/shard_map/reshape | solution.py:671
  55.3 0.7 %copy.22 = bf16[1024,128]{1,0:T(8,128)(2,1)} copy(bf16[1024,128]{1,0:T(8,128)(2,1)S(1)} %get-tuple-element.28) | data formatting | bytes 524288
  56.0 0.7 %copy.23 = bf16[1024,128]{1,0:T(8,128)(2,1)} copy(bf16[1024,128]{1,0:T(8,128)(2,1)S(1)} %get-tuple-element.29) | data formatting | bytes 524288
  56.7 0.7 %copy.24 = bf16[1024,128]{1,0:T(8,128)(2,1)} copy(bf16[1024,128]{1,0:T(8,128)(2,1)S(1)} %get-tuple-element.30) | data formatting | bytes 524288
  57.4 0.7 %copy.25 = bf16[1024,128]{1,0:T(8,128)(2,1)} copy(bf16[1024,128]{1,0:T(8,128)(2,1)S(1)} %get-tuple-element.31) | data formatting | bytes 524288
  (2 shorter events, 0.0 us)
Async XLA Ops:
  0.6 0.9 %copy-start.4 = (f32[64,16]{0,1:T(8,128)S(1)}, f32[64,16]{0,1:T(8,128)}, u32[]{:S(2)}) copy-start(f32[64,16]{0,1:T(8,128)} %param.11) | copy-start | bytes 12292
  0.6 0.9 %copy-start.5 = (f32[64,16]{0,1:T(8,128)S(1)}, f32[64,16]{0,1:T(8,128)}, u32[]{:S(2)}) copy-start(f32[64,16]{0,1:T(8,128)} %param.12) | copy-start | bytes 12292
  1.7 1.0 %copy-start = (bf16[1024,128]{1,0:T(8,128)(2,1)S(1)}, bf16[1024,128]{1,0:T(8,128)(2,1)}, u32[]{:S(2)}) copy-start(bf16[1024,128]{1,0:T(8,128)(2,1)} %query_ref.1) | copy-start | bytes 786436
  2.6 0.9 %copy-start.1 = (bf16[1024,128]{1,0:T(8,128)(2,1)S(1)}, bf16[1024,128]{1,0:T(8,128)(2,1)}, u32[]{:S(2)}) copy-start(bf16[1024,128]{1,0:T(8,128)(2,1)} %key_ref.1) | copy-start | bytes 786436
  3.6 0.9 %copy-start.2 = (bf16[1024,128]{1,0:T(8,128)(2,1)S(1)}, bf16[1024,128]{1,0:T(8,128)(2,1)}, u32[]{:S(2)}) copy-start(bf16[1024,128]{1,0:T(8,128)(2,1)} %value_ref.1) | copy-start | bytes 786436
  4.5 0.9 %copy-start.3 = (bf16[1024,128]{1,0:T(8,128)(2,1)S(1)}, bf16[1024,128]{1,0:T(8,128)(2,1)}, u32[]{:S(2)}) copy-start(bf16[1024,128]{1,0:T(8,128)(2,1)} %grad_ref.1) | copy-start | bytes 786436
where the time goes:
time: 58.4 us; the launch traced here: 58.1 us
  Pallas kernels  48.3 us (83%)
  local copies, waits for them, and re-layouts  9.01 us (15%)
  between operations  0.71 us (1%)
    pallas_call x1, Pallas kernels, local(): pl.pallas_call(functools.partial(layer_kernel, n, modes, tokens, scale),...  48.3 us
    unnamed x16, local copies, waits for them, and re-layouts  6.62 us

commit v1 on v0

--- a/solution.py
+++ b/solution.py
@@ -245,61 +245,73 @@
 def layer_kernel(
     n, modes, tokens, scale,
     query_ref, key_ref, value_ref, grad_ref, weight_ref, param_ref,
-    out_ref, gq_ref, gk_ref, gv_ref, short_ref, modal_ref,
-    streams, hats, mixed, gmixed, conv, conv_back, prod, cots,
-    params, decay, gain, rate,
-    fwd_send, fwd_recv, bwd_send, bwd_recv, acc_send, acc_recv,
-    carry_send, carry_recv, modal_send, modal_recv,
-    short_send, short_recv, total_send, total_recv,
-    send_sem, recv_sem, halo_send, halo_recv,
+    out_ref, gq_ref, gk_ref, gv_ref, short_ref, res_ref, log_ref,
+    inputs, streams, hats, mixed, gmixed, conv, conv_back, prod, cots,
+    weights, params, decay, gain, rate,
+    edge_send, edge_recv, acc_send, acc_recv, carry_send, carry_recv,
+    modal_send, modal_recv, short_send, short_recv, total_send, total_recv,
+    load_sem, send_sem, recv_sem, halo_send, halo_recv,
 ):
     me = lax.axis_index("seq")
     extent = tokens + HALO
+    rows_all = 3 * TAPS
+    owners = (rows_all + 1) // 2
     f32 = jnp.float32
     zero = jnp.zeros((SUB, LANE), f32)
 
     def rounded(value):
         return value.astype(jnp.bfloat16).astype(f32)
 
-    def exchange(phase, k, source, target):
-        peer = lax.rem(me + k, n)
-        return pltpu.make_async_remote_copy(
-            src_ref=source(peer),
-            dst_ref=target(me),
-            send_sem=send_sem.at[phase, k],
-            recv_sem=recv_sem.at[phase, k],
+    def tree(parts):
+        while len(parts) > 1:
+            parts = [parts[i] + parts[i + 1] for i in range(0, len(parts), 2)]
+        return parts[0]
+
+    def per_mode(ref):
+        return [ref[m * SUB : (m + 1) * SUB, :] for m in range(modes)]
+
+    loads = [
+        pltpu.make_async_copy(ref, inputs.at[s], load_sem.at[s])
+        for s, ref in enumerate((query_ref, key_ref, value_ref, grad_ref))
+    ]
+    for load in loads:
+        load.start()
+
+    barrier = pltpu.get_barrier_semaphore()
+    peers = [lax.rem(me + k, n) for k in range(1, n)]
+    for peer in peers:
+        pl.semaphore_signal(
+            barrier, inc=1, device_id={"seq": peer}, device_id_type=MESH
+        )
+
+    def send(phase, peer, source, target):
+        pltpu.make_async_remote_copy(
+            src_ref=source,
+            dst_ref=target,
+            send_sem=send_sem.at[phase],
+            recv_sem=recv_sem.at[phase],
             device_id={"seq": peer},
             device_id_type=MESH,
-        )
-
-    def start_all(phase, source, target):
-        def step(k, carry):
-            exchange(phase, k, source, target).start()
-            return carry
-
-        lax.fori_loop(1, n, step, 0)
-
-    def wait_all(phase, source, target):
-        def step(k, carry):
-            exchange(phase, k, source, target).wait()
-            return carry
-
-        lax.fori_loop(1, n, step, 0)
-
-    barrier = pltpu.get_barrier_semaphore()
-
-    def greet(k, carry):
-        pl.semaphore_signal(
-            barrier, inc=1, device_id={"seq": lax.rem(me + k, n)}, device_id_type=MESH
-        )
-        return carry
-
-    lax.fori_loop(1, n, greet, 0)
-
-    ins = (query_ref, key_ref, value_ref, grad_ref)
+        ).start()
+
+    def sent(phase, like):
+        pltpu.make_async_copy(like, like, send_sem.at[phase]).wait()
+
+    def arrived(phase, like):
+        pltpu.make_async_copy(like, like, recv_sem.at[phase]).wait()
+
+    others = pl.ds(0, n - 1)
+
+    for s in range(3):
+        for b in range(SUB):
+            weights[pl.ds(s * TAPS * SUB + b, TAPS, stride=SUB), :] = weight_ref[
+                s, :, b * LANE : (b + 1) * LANE
+            ]
+
     for s in range(4):
+        loads[s].wait()
         for b in range(SUB):
-            block = ins[s][b * LANE : (b + 1) * LANE, :].astype(f32)
+            block = inputs[s, b * LANE : (b + 1) * LANE, :].astype(f32)
             streams[s, pl.ds(HALO * SUB + b, tokens, stride=SUB), :] = block.T
 
     pl.semaphore_wait(barrier, n - 1)
@@ -339,13 +351,14 @@
     def _():
         streams[:, edge + last : 2 * edge + last, :] = jnp.zeros((4, edge, LANE), f32)
 
-    own_rows = pl.ds(pl.multiple_of(me * modes, modes), modes)
-    par_src = lambda peer: param_ref
-    par_dst = lambda owner: params.at[pl.ds(pl.multiple_of(owner * modes, modes), modes)]
-    start_all(0, par_src, par_dst)
-    params[own_rows, :] = param_ref[...]
-
-    taps = [[weight_ref[s * TAPS + j] for j in range(TAPS)] for s in range(3)]
+    for peer in peers:
+        send(0, peer, param_ref, params.at[me])
+    params[me] = param_ref[...]
+
+    taps = [
+        [weights[(s * TAPS + j) * SUB : (s * TAPS + j + 1) * SUB, :] for j in range(TAPS)]
+        for s in range(3)
+    ]
 
     def filter_token(t):
         vals = []
@@ -381,11 +394,11 @@
     token_loop(0, HALO, 2, filter_token)
     token_loop(tokens, extent, 2, filter_token)
 
-    wait_all(0, par_src, par_dst)
+    arrived(0, params.at[others])
     low_half = lax.broadcasted_iota(jnp.int32, (SUB, LANE), 1) < LANE // 2
     for m in range(modes):
-        even = params[pl.ds(m, SUB, stride=2 * modes), :]
-        odd = params[pl.ds(modes + m, SUB, stride=2 * modes), :]
+        even = jnp.concatenate([params[2 * b, m : m + 1, :] for b in range(SUB)], axis=0)
+        odd = jnp.concatenate([params[2 * b + 1, m : m + 1, :] for b in range(SUB)], axis=0)
         log_rate = jnp.where(low_half, even, pltpu.roll(odd, LANE // 2, 1))
         residue = jnp.where(low_half, pltpu.roll(even, LANE // 2, 1), odd)
         r = jnp.exp(log_rate)
@@ -394,6 +407,27 @@
         gain[slab(m), :] = residue * jnp.sqrt(2.0 * r)
 
     UN = 4
+    decays = per_mode(decay)
+
+    def edge_step(i, carry):
+        x, z = [list(c) for c in carry]
+        for u in range(UN):
+            t = i * UN + u
+            value = mixed[slab(t), :]
+            cot = gmixed[slab(tokens - 1 - t), :]
+            for m in range(modes):
+                x[m] = decays[m] * x[m] + value
+                z[m] = decays[m] * z[m] + cot
+        return tuple(x), tuple(z)
+
+    x, z = lax.fori_loop(0, tokens // UN, edge_step, ((zero,) * modes,) * 2)
+    for m in range(modes):
+        edge_send[m, 0:SUB, :] = x[m]
+        edge_send[m, SUB : 2 * SUB, :] = z[m]
+    for peer in peers:
+        send(1, peer, edge_send.at[peer], edge_recv.at[me])
+    edge_recv[me] = edge_send[me]
+
     for first in range(0, modes, GROUP):
         group = range(first, first + GROUP)
 
@@ -403,24 +437,24 @@
                 t = i * UN + u
                 value = mixed[slab(t), :]
                 cot = gmixed[slab(t), :]
-                total = conv[slab(t), :] if first else zero
+                parts = []
                 for p, m in enumerate(group):
                     a = decay[m * SUB : (m + 1) * SUB, :]
                     y[p] = a * (y[p] + x[p])
                     x[p] = a * x[p] + value
-                    total = total + gain[m * SUB : (m + 1) * SUB, :] * x[p]
+                    parts.append(gain[m * SUB : (m + 1) * SUB, :] * x[p])
                     ax[p] = ax[p] + cot * x[p]
                     ay[p] = ay[p] + cot * y[p]
-                conv[slab(t), :] = total
+                total = tree(parts)
+                conv[slab(t), :] = conv[slab(t), :] + total if first else total
             return tuple(tuple(c) for c in (x, y, ax, ay))
 
         zeros = tuple(zero for _ in group)
         x, y, ax, ay = lax.fori_loop(0, tokens // UN, fwd_step, (zeros,) * 4)
         for p, m in enumerate(group):
-            fwd_send[m, 0:SUB, :] = x[p]
-            fwd_send[m, SUB : 2 * SUB, :] = y[p]
-            acc_send[m, 0:SUB, :] = ax[p]
-            acc_send[m, SUB : 2 * SUB, :] = ay[p]
+            acc_send[m, 0:SUB, :] = y[p]
+            acc_send[m, 2 * SUB : 3 * SUB, :] = ax[p]
+            acc_send[m, 3 * SUB : 4 * SUB, :] = ay[p]
         x = list(x)
         for t in range(tokens, extent):
             value = mixed[t * SUB : (t + 1) * SUB, :]
@@ -430,9 +464,21 @@
                 total = total + gain[m * SUB : (m + 1) * SUB, :] * x[p]
             conv[t * SUB : (t + 1) * SUB, :] = total
 
-    fwd_src = lambda peer: fwd_send.at[peer]
-    fwd_dst = lambda owner: fwd_recv.at[owner]
-    start_all(1, fwd_src, fwd_dst)
+    my_rate = rate[slab(me), :]
+    my_decay = decay[slab(me), :]
+    my_gain = gain[slab(me), :]
+    whole = jnp.exp(-float(tokens) * my_rate)
+    arrived(1, edge_recv.at[others])
+    h, z = zero, zero
+    for d in range(n):
+        back = n - 1 - d
+        carry_send[d, 0:SUB, :] = h
+        carry_send[back, SUB : 2 * SUB, :] = z
+        h = whole * h + edge_recv[d, 0:SUB, :]
+        z = whole * z + edge_recv[back, SUB : 2 * SUB, :]
+    for peer in peers:
+        send(2, peer, carry_send.at[peer], carry_recv.at[me])
+    carry_recv[me] = carry_send[me]
 
     for first in range(0, modes, GROUP):
         group = range(first, first + GROUP)
@@ -442,96 +488,39 @@
             for u in range(UN):
                 t = tokens - 1 - (i * UN + u)
                 cot = gmixed[slab(t), :]
-                total = conv_back[slab(t), :] if first else zero
+                parts = []
                 for p, m in enumerate(group):
                     a = decay[m * SUB : (m + 1) * SUB, :]
                     z[p] = a * z[p] + cot
                     w[p] = a * w[p] + z[p]
-                    total = total + gain[m * SUB : (m + 1) * SUB, :] * z[p]
-                conv_back[slab(t), :] = total
+                    parts.append(gain[m * SUB : (m + 1) * SUB, :] * z[p])
+                total = tree(parts)
+                conv_back[slab(t), :] = conv_back[slab(t), :] + total if first else total
             return tuple(tuple(c) for c in (z, w))
 
         zeros = tuple(zero for _ in group)
         z, w = lax.fori_loop(0, tokens // UN, bwd_step, (zeros,) * 2)
         for p, m in enumerate(group):
-            bwd_send[m, 0:SUB, :] = z[p]
-            bwd_send[m, SUB : 2 * SUB, :] = w[p]
-
-    bwd_src = lambda peer: bwd_send.at[peer]
-    bwd_dst = lambda owner: bwd_recv.at[owner]
-    start_all(2, bwd_src, bwd_dst)
-    acc_src = lambda peer: acc_send.at[peer]
-    acc_dst = lambda owner: acc_recv.at[owner]
-    start_all(3, acc_src, acc_dst)
-
-    fwd_recv[me] = fwd_send[me]
-    bwd_recv[me] = bwd_send[me]
+            acc_send[m, SUB : 2 * SUB, :] = w[p]
+
+    for peer in peers:
+        send(3, peer, acc_send.at[peer], acc_recv.at[me])
     acc_recv[me] = acc_send[me]
-    my_rate = rate[slab(me), :]
-    my_decay = decay[slab(me), :]
-    my_gain = gain[slab(me), :]
-    whole = jnp.exp(-float(tokens) * my_rate)
-    wait_all(1, fwd_src, fwd_dst)
-
-    def scan_fwd(d, h):
-        carry_send[d, 0:SUB, :] = h
-        return whole * h + fwd_recv[d, 0:SUB, :]
-
-    lax.fori_loop(0, n, scan_fwd, zero)
-    wait_all(2, bwd_src, bwd_dst)
-
-    def scan_bwd(i, z):
-        d = n - 1 - i
-        carry_send[d, SUB : 2 * SUB, :] = z
-        return whole * z + bwd_recv[d, 0:SUB, :]
-
-    lax.fori_loop(0, n, scan_bwd, zero)
-    carry_src = lambda peer: carry_send.at[peer]
-    carry_dst = lambda owner: carry_recv.at[owner]
-    start_all(4, carry_src, carry_dst)
-    carry_recv[me] = carry_send[me]
-
-    wait_all(3, acc_src, acc_dst)
-
-    def scan_acc(d, carry):
-        hy, acc_x, acc_y = carry
-        h = carry_send[d, 0:SUB, :]
-        z0 = my_decay * bwd_recv[d, 0:SUB, :]
-        z1 = my_decay * bwd_recv[d, SUB : 2 * SUB, :]
-        acc_x = acc_x + (acc_recv[d, 0:SUB, :] + h * z0)
-        acc_y = acc_y + (acc_recv[d, SUB : 2 * SUB, :] + h * z1 + hy * z0)
-        hy = whole * (hy + float(tokens) * h) + fwd_recv[d, SUB : 2 * SUB, :]
-        return hy, acc_x, acc_y
-
-    _, acc_x, acc_y = lax.fori_loop(0, n, scan_acc, (zero, zero, zero))
-    modal_send[0:SUB, :] = acc_x * jnp.sqrt(2.0 * my_rate) * scale
-    modal_send[SUB : 2 * SUB, :] = my_gain * (0.5 * acc_x - my_rate * acc_y) * scale
-    modal_src = lambda peer: modal_send
-    modal_dst = lambda owner: modal_recv.at[owner]
-    start_all(5, modal_src, modal_dst)
-    modal_recv[me] = modal_send[...]
-
-    wait_all(4, carry_src, carry_dst)
-
-    def finish_fwd(t, c):
-        c = [decay[m * SUB : (m + 1) * SUB, :] * c[m] for m in range(modes)]
-        parts = c
-        while len(parts) > 1:
-            parts = [parts[i] + parts[i + 1] for i in range(0, len(parts), 2)]
-        total = rounded(conv[slab(t), :] + parts[0])
-        prod[slab(t), :] = hats[0, slab(t), :] * total
-        cots[0, slab(t), :] = streams[3, slab(t + HALO), :] * total
-        return c
+
+    arrived(2, carry_recv.at[others])
+    gains = per_mode(gain)
 
     def fwd_two(i, c):
         c = list(c)
         for u in range(2):
-            c = finish_fwd(i * 2 + u, c)
+            t = i * 2 + u
+            c = [decays[m] * c[m] for m in range(modes)]
+            total = rounded(conv[slab(t), :] + tree(c))
+            prod[slab(t), :] = hats[0, slab(t), :] * total
+            cots[0, slab(t), :] = streams[3, slab(t + HALO), :] * total
         return tuple(c)
 
-    start = tuple(
-        gain[m * SUB : (m + 1) * SUB, :] * carry_recv[m, 0:SUB, :] for m in range(modes)
-    )
+    start = tuple(gains[m] * carry_recv[m, 0:SUB, :] for m in range(modes))
     lax.fori_loop(0, extent // 2, fwd_two, start)
 
     def store_back(t, total):
@@ -543,32 +532,22 @@
         c = list(c)
         for u in range(2):
             t = tokens - 1 - (i * 2 + u)
-            c = [decay[m * SUB : (m + 1) * SUB, :] * c[m] for m in range(modes)]
-            parts = c
-            while len(parts) > 1:
-                parts = [parts[k] + parts[k + 1] for k in range(0, len(parts), 2)]
-            store_back(t, conv_back[slab(t), :] + parts[0])
+            c = [decays[m] * c[m] for m in range(modes)]
+            store_back(t, conv_back[slab(t), :] + tree(c))
         return tuple(c)
 
-    start = tuple(
-        gain[m * SUB : (m + 1) * SUB, :] * carry_recv[m, SUB : 2 * SUB, :]
-        for m in range(modes)
-    )
+    start = tuple(gains[m] * carry_recv[m, SUB : 2 * SUB, :] for m in range(modes))
     lax.fori_loop(0, tokens // 2, bwd_two, start)
 
-    for h in range(HALO):
-        conv_back[(tokens + h) * SUB : (tokens + h + 1) * SUB, :] = zero
+    ahead = [zero] * HALO
     for m in range(modes):
         grow = jnp.exp(rate[m * SUB : (m + 1) * SUB, :])
         z = carry_recv[m, SUB : 2 * SUB, :]
-        weight = gain[m * SUB : (m + 1) * SUB, :]
         for h in range(HALO):
-            rows = slice((tokens + h) * SUB, (tokens + h + 1) * SUB)
-            conv_back[rows, :] = conv_back[rows, :] + weight * z
-            z = grow * (z - gmixed[rows, :])
+            ahead[h] = ahead[h] + gains[m] * z
+            z = grow * (z - gmixed[(tokens + h) * SUB : (tokens + h + 1) * SUB, :])
     for h in range(HALO):
-        t = tokens + h
-        store_back(t, conv_back[t * SUB : (t + 1) * SUB, :])
+        store_back(tokens + h, ahead[h])
 
     def short_step(i, accs):
         accs = list(accs)
@@ -581,15 +560,38 @@
                     accs[at] = accs[at] + cot * streams[s, slab(t + HALO - j), :]
         return tuple(accs)
 
-    accs = lax.fori_loop(0, tokens // 2, short_step, (zero,) * (3 * TAPS))
-    for row in range(2 * n):
+    accs = lax.fori_loop(0, tokens // 2, short_step, (zero,) * rows_all)
+    for row in range(2 * owners):
         short_send[row // 2, (row % 2) * SUB : (row % 2 + 1) * SUB, :] = (
-            accs[row] if row < 3 * TAPS else zero
+            accs[row] if row < rows_all else zero
         )
-    short_src = lambda peer: short_send.at[peer]
-    short_dst = lambda owner: short_recv.at[owner]
-    start_all(6, short_src, short_dst)
-    short_recv[me] = short_send[me]
+    for peer in peers:
+
+        @pl.when(peer < owners)
+        def _(peer=peer):
+            send(5, peer, short_send.at[peer], short_recv.at[me])
+
+    @pl.when(me < owners)
+    def _():
+        short_recv[me] = short_send[me]
+
+    arrived(3, acc_recv.at[others])
+    hy, acc_x, acc_y = zero, zero, zero
+    for d in range(n):
+        h = carry_send[d, 0:SUB, :]
+        z0 = my_decay * edge_recv[d, SUB : 2 * SUB, :]
+        z1 = my_decay * acc_recv[d, SUB : 2 * SUB, :]
+        acc_x = acc_x + (acc_recv[d, 2 * SUB : 3 * SUB, :] + h * z0)
+        acc_y = acc_y + (acc_recv[d, 3 * SUB : 4 * SUB, :] + h * z1 + hy * z0)
+        hy = whole * (hy + float(tokens) * h) + acc_recv[d, 0:SUB, :]
+    grad_res = acc_x * jnp.sqrt(2.0 * my_rate) * scale
+    grad_log = my_gain * (0.5 * acc_x - my_rate * acc_y) * scale
+    for b in range(SUB):
+        modal_send[b, 0:1, :] = grad_res[b : b + 1, :]
+        modal_send[b, 1:2, :] = grad_log[b : b + 1, :]
+    for peer in peers:
+        send(4, peer, modal_send.at[lax.div(peer, 2)], modal_recv.at[me])
+    modal_recv[me] = modal_send[lax.div(me, 2)]
 
     def taps_step(t):
         for s in range(3):
@@ -600,28 +602,67 @@
 
     token_loop(0, tokens, 2, taps_step)
 
-    wait_all(6, short_src, short_dst)
-    total = short_recv[0]
-    for d in range(1, n):
-        total = total + short_recv[d]
-    total_send[...] = total * scale
-    total_src = lambda peer: total_send
-    total_dst = lambda owner: total_recv.at[owner]
-    start_all(7, total_src, total_dst)
-    total_recv[me] = total_send[...]
-
-    for b in range(SUB):
-        rows = slice(b * LANE, (b + 1) * LANE)
-        out_ref[rows, :] = prod[pl.ds(b, tokens, stride=SUB), :].T.astype(jnp.bfloat16)
-    for s, ref in enumerate((gq_ref, gk_ref, gv_ref)):
+    @pl.when(me < owners)
+    def _():
+        arrived(5, short_recv.at[others])
+        total = short_recv[0]
+        for d in range(1, n):
+            total = total + short_recv[d]
+        total_send[...] = total * scale
+        for peer in peers:
+            send(6, peer, total_send, total_recv.at[me])
+        total_recv[me] = total_send[...]
+
+    for s, ref in enumerate((out_ref, gq_ref, gk_ref, gv_ref)):
         for b in range(SUB):
-            rows = slice(b * LANE, (b + 1) * LANE)
-            ref[rows, :] = hats[s, pl.ds(b, tokens, stride=SUB), :].T.astype(jnp.bfloat16)
-
-    wait_all(5, modal_src, modal_dst)
-    modal_ref[...] = modal_recv[...]
-    wait_all(7, total_src, total_dst)
-    short_ref[...] = total_recv[...]
+            rows = pl.ds(b, tokens, stride=SUB)
+            block = hats[s - 1, rows, :] if s else prod[rows, :]
+            ref[b * LANE : (b + 1) * LANE, :] = block.T.astype(jnp.bfloat16)
+
+    arrived(4, modal_recv.at[others])
+    odd_owner = lax.rem(me, 2) == 1
+    for at, ref in ((0, res_ref), (1, log_ref)):
+        table = jnp.concatenate([modal_recv[m, at : at + 1, :] for m in range(modes)], axis=0)
+        table = jnp.where(odd_owner, pltpu.roll(table, LANE // 2, 1), table)
+        ref[...] = table[:, : LANE // 2]
+
+    @pl.when(me < owners)
+    def _():
+        arrived(6, total_recv.at[pl.ds(0, owners - 1)])
+        sent(5, short_recv.at[pl.ds(0, owners - 1)])
+        sent(6, short_recv.at[others])
+
+    @pl.when(me >= owners)
+    def _():
+        arrived(6, total_recv)
+        sent(5, short_recv.at[pl.ds(0, owners)])
+
+    for s in range(3):
+        for b in range(SUB):
+            for j in range(TAPS):
+                row = s * TAPS + j
+                at = (row % 2) * SUB + b
+                short_ref[s, j : j + 1, b * LANE : (b + 1) * LANE] = total_recv[
+                    row // 2, at : at + 1, :
+                ]
+
+    sent(0, params.at[others])
+    sent(1, edge_recv.at[others])
+    sent(2, carry_recv.at[others])
+    sent(3, acc_recv.at[others])
+    sent(4, modal_recv.at[others])
+
+
+def hand_over(*refs):
+    sems = refs[-1]
+    count = (len(refs) - 1) // 2
+    copies = [
+        pltpu.make_async_copy(refs[i], refs[count + i], sems.at[i]) for i in range(count)
+    ]
+    for copy in copies:
+        copy.start()
+    for copy in copies:
+        copy.wait()
 
 
 def local(query_in, key_in, value_in, short_weight, residue, log_rate, grad_out):
@@ -636,42 +677,59 @@
     scale = 1.0 / math.sqrt(tokens * n)
     f32 = jnp.float32
     rows = (tokens + HALO) * SUB
-    weight = short_weight.reshape(3 * TAPS, SUB, LANE)
+    owners = (3 * TAPS + 1) // 2
     param = jnp.concatenate([log_rate.T, residue.T], axis=1)
     vmem = pl.BlockSpec(memory_space=pltpu.VMEM)
-    stage = pltpu.VMEM((n, 2 * SUB, LANE), f32)
+    hbm = pl.BlockSpec(memory_space=pltpu.MemorySpace.HBM)
+    pair = pltpu.VMEM((n, 2 * SUB, LANE), f32)
+    quad = pltpu.VMEM((n, 4 * SUB, LANE), f32)
     flat = pltpu.VMEM((rows, LANE), f32)
+    triple = pltpu.VMEM((3, rows, LANE), f32)
     small = pltpu.VMEM((modes * SUB, LANE), f32)
     shape = jax.ShapeDtypeStruct((width, tokens), jnp.bfloat16)
-    table = jax.ShapeDtypeStruct((n, 2 * SUB, LANE), f32)
-    out, gq, gk, gv, short, modal = pl.pallas_call(
+    modal = jax.ShapeDtypeStruct((modes, own), f32)
+    results = pl.pallas_call(
         functools.partial(layer_kernel, n, modes, tokens, scale),
-        out_shape=(shape, shape, shape, shape, table, table),
-        in_specs=[vmem] * 6,
-        out_specs=(vmem,) * 6,
+        out_shape=(
+            shape, shape, shape, shape,
+            jax.ShapeDtypeStruct(short_weight.shape, f32), modal, modal,
+        ),
+        in_specs=[hbm] * 4 + [vmem] * 2,
+        out_specs=(vmem,) * 7,
         scratch_shapes=[
+            pltpu.VMEM((4, width, tokens), jnp.bfloat16),
             pltpu.VMEM((4, rows + HALO * SUB, LANE), f32),
-            pltpu.VMEM((3, rows, LANE), f32),
-            flat, flat, flat, flat, flat,
-            pltpu.VMEM((3, rows, LANE), f32),
-            pltpu.VMEM((n * modes, LANE), f32),
+            triple, flat, flat, flat, flat, flat, triple,
+            pltpu.VMEM((3 * TAPS * SUB, LANE), f32),
+            pltpu.VMEM((n, modes, LANE), f32),
             small, small, small,
-            stage, stage, stage, stage, stage, stage,
-            stage, stage, pltpu.VMEM((2 * SUB, LANE), f32), stage,
-            stage, stage, pltpu.VMEM((2 * SUB, LANE), f32), stage,
-            pltpu.SemaphoreType.DMA((8, n)),
-            pltpu.SemaphoreType.DMA((8, n)),
+            pair, pair, quad, quad, pair, pair,
+            pltpu.VMEM((SUB, 2, LANE), f32),
+            pltpu.VMEM((n, 2, LANE), f32),
+            pltpu.VMEM((owners, 2 * SUB, LANE), f32),
+            pair,
+            pltpu.VMEM((2 * SUB, LANE), f32),
+            pltpu.VMEM((owners, 2 * SUB, LANE), f32),
+            pltpu.SemaphoreType.DMA((4,)),
+            pltpu.SemaphoreType.DMA((7,)),
+            pltpu.SemaphoreType.DMA((7,)),
             pltpu.SemaphoreType.DMA((2,)),
             pltpu.SemaphoreType.DMA((2,)),
         ],
         compiler_params=pltpu.CompilerParams(
-            collective_id=0, has_side_effects=True, vmem_limit_bytes=40 * 2**20
+            collective_id=0, has_side_effects=True, vmem_limit_bytes=56 * 2**20
         ),
-    )(query_in, key_in, value_in, grad_out, weight, param)
-    short = short.reshape(2 * n, width)[: 3 * TAPS].reshape(3, TAPS, width)
-    modal = modal.reshape(modes, 2, width)
-    mine = lax.dynamic_slice_in_dim(modal, lax.axis_index("seq") * own, own, 2)
-    return (out, gq, gk, gv, short, mine[:, 0].T, mine[:, 1].T)
+    )(query_in, key_in, value_in, grad_out, short_weight, param)
+    count = len(results)
+    results = pl.pallas_call(
+        hand_over,
+        out_shape=[jax.ShapeDtypeStruct(r.shape, r.dtype) for r in results],
+        in_specs=[hbm] * count,
+        out_specs=[hbm] * count,
+        scratch_shapes=[pltpu.SemaphoreType.DMA((count,))],
+        compiler_params=pltpu.CompilerParams(vmem_limit_bytes=60 * 2**20),
+    )(*results)
+    return (*results[:5], results[5].T, results[6].T)
 
 
 def solution(mesh):

time: 58.4 us -> 78.7 us (1.35)
  Pallas kernels: 48.3 us -> 76.4 us
  local copies, waits for them, and re-layouts: 9.01 us -> 0 us
  other arithmetic: 0.08 us -> 1.39 us
    pallas_call x0 -> x1, Pallas kernels: none -> 36.4 us  [local(): pl.pallas_call(hand_over, out_shape=[jax.ShapeDtypeStruct(r.shape, r.dtyp...]
    pallas_call x1, Pallas kernels: 48.3 us -> 40 us  [local(): pl.pallas_call(functools.partial(layer_kernel, n, modes, tokens, scale),...]
    unnamed x16 -> x0, local copies, waits for them, and re-layouts: 6.62 us -> none
    reshape x4 -> x0, local copies, waits for them, and re-layouts: 1.67 us -> none  [the longest x1 0.92 us: local(): weight = short_weight.reshape(3 * TAPS, SUB, LANE)]
    concatenate x1, other arithmetic: 0.08 us -> 1.39 us  [local(): param = jnp.concatenate([log_rate.T, residue.T], axis=1)]
where the time goes in v1:
time: 78.7 us; the launch traced here: 78.4 us
  Pallas kernels  76.4 us (97%)
  other arithmetic  1.39 us (2%)
    pallas_call x1, Pallas kernels, local(): pl.pallas_call(functools.partial(layer_kernel, n, modes, tokens, scale),...  40 us
    pallas_call x1, Pallas kernels, local(): pl.pallas_call(hand_over, out_shape=[jax.ShapeDtypeStruct(r.shape, r.dtyp...  36.4 us

profile of v1, /device:TPU:0, one launch (start us, length us, event | category | flops | bytes accessed | tf_op | source)
XLA Modules:
  0.0 78.4 jit_solution(16108189777634219099)
XLA Ops:
  0.6 1.4 %pad_maximum_fusion.param_ref = f32[16,128]{1,0:T(8,128)} fusion(f32[16,64]{1,0:T(8,128)} %bitcast.4, f32[16,64]{1,0:T(8,128)} %bitcast.5), kind=kLoop, calls=%fused_computation | loop fusion | flops 2048 | bytes 16384 | tf_op jit(solution)/shard_map/concatenate | solution.py:681
  2.0 40.0 %shard_map.126 = (bf16[1024,128]{1,0:T(8,128)(2,1)}, bf16[1024,128]{1,0:T(8,128)(2,1)}, bf16[1024,128]{1,0:T(8,128)(2,1)}, bf16[1024,128]{1,0:T(8,128)(2,1)}, f3...) custom-call(bf16[1024,128]{1,0:T(8,128)(2,1)} %query_ref.1, bf16[1024,128]{1,0:T(8,128)(2,1)} %key_ref.1, ...), custom_call_target="tpu_custom_call" | custom-call | tf_op jit(solution)/shard_map/pallas_call | solution.py:691
  42.0 36.4 %shard_map.127 = (bf16[1024,128]{1,0:T(8,128)(2,1)}, bf16[1024,128]{1,0:T(8,128)(2,1)}, bf16[1024,128]{1,0:T(8,128)(2,1)}, bf16[1024,128]{1,0:T(8,128)(2,1)}, f3...) custom-call(bf16[1024,128]{1,0:T(8,128)(2,1)} %get-tuple-element.21.refs_0_, ...), custom_call_target="tpu_custom_call" | custom-call | tf_op jit(solution)/shard_map/pallas_call | solution.py:724

commit v2 on v1

--- a/solution.py
+++ b/solution.py
@@ -246,11 +246,11 @@
     n, modes, tokens, scale,
     query_ref, key_ref, value_ref, grad_ref, weight_ref, param_ref,
     out_ref, gq_ref, gk_ref, gv_ref, short_ref, res_ref, log_ref,
-    inputs, streams, hats, mixed, gmixed, conv, conv_back, prod, cots,
+    inputs, results, streams, hats, mixed, gmixed, conv, conv_back, prod, cots,
     weights, params, decay, gain, rate,
-    edge_send, edge_recv, acc_send, acc_recv, carry_send, carry_recv,
-    modal_send, modal_recv, short_send, short_recv, total_send, total_recv,
-    load_sem, send_sem, recv_sem, halo_send, halo_recv,
+    edge_send, edge_recv, acc_hold, acc_send, acc_recv,
+    carry_hold, carry_send, carry_recv, modal_send, modal_recv, short_send, short_recv, total_send, total_recv,
+    load_sem, store_sem, send_sem, recv_sem, halo_send, halo_recv,
 ):
     me = lax.axis_index("seq")
     extent = tokens + HALO
@@ -308,13 +308,29 @@
                 s, :, b * LANE : (b + 1) * LANE
             ]
 
+    eye = (
+        lax.broadcasted_iota(jnp.int32, (LANE, LANE), 0)
+        == lax.broadcasted_iota(jnp.int32, (LANE, LANE), 1)
+    ).astype(jnp.bfloat16)
+
+    def turned(block):
+        return lax.dot_general(
+            eye, block, (((1,), (1,)), ((), ())), preferred_element_type=f32
+        )
+
     for s in range(4):
         loads[s].wait()
-        for b in range(SUB):
-            block = inputs[s, b * LANE : (b + 1) * LANE, :].astype(f32)
-            streams[s, pl.ds(HALO * SUB + b, tokens, stride=SUB), :] = block.T
-
-    pl.semaphore_wait(barrier, n - 1)
+        for b in range(0, SUB, 2):
+            block = turned(inputs[s, b * LANE : (b + 2) * LANE, :])
+            for half in range(2):
+                streams[s, pl.ds(HALO * SUB + b + half, tokens, stride=SUB), :] = block[
+                    :, half * LANE : (half + 1) * LANE
+                ]
+        if s == 1:
+            pl.semaphore_wait(barrier, n - 1)
+            for peer in peers:
+                send(0, peer, param_ref, params.at[me])
+            params[me] = param_ref[...]
 
     edge = HALO * SUB
     last = tokens * SUB
@@ -350,10 +366,6 @@
     @pl.when(me == n - 1)
     def _():
         streams[:, edge + last : 2 * edge + last, :] = jnp.zeros((4, edge, LANE), f32)
-
-    for peer in peers:
-        send(0, peer, param_ref, params.at[me])
-    params[me] = param_ref[...]
 
     taps = [
         [weights[(s * TAPS + j) * SUB : (s * TAPS + j + 1) * SUB, :] for j in range(TAPS)]
@@ -422,8 +434,7 @@
 
     x, z = lax.fori_loop(0, tokens // UN, edge_step, ((zero,) * modes,) * 2)
     for m in range(modes):
-        edge_send[m, 0:SUB, :] = x[m]
-        edge_send[m, SUB : 2 * SUB, :] = z[m]
+        edge_send[m] = jnp.concatenate([x[m], z[m]], axis=0).astype(jnp.bfloat16)
     for peer in peers:
         send(1, peer, edge_send.at[peer], edge_recv.at[me])
     edge_recv[me] = edge_send[me]
@@ -452,9 +463,9 @@
         zeros = tuple(zero for _ in group)
         x, y, ax, ay = lax.fori_loop(0, tokens // UN, fwd_step, (zeros,) * 4)
         for p, m in enumerate(group):
-            acc_send[m, 0:SUB, :] = y[p]
-            acc_send[m, 2 * SUB : 3 * SUB, :] = ax[p]
-            acc_send[m, 3 * SUB : 4 * SUB, :] = ay[p]
+            acc_hold[m, 0:SUB, :] = y[p]
+            acc_hold[m, 2 * SUB : 3 * SUB, :] = ax[p]
+            acc_hold[m, 3 * SUB : 4 * SUB, :] = ay[p]
         x = list(x)
         for t in range(tokens, extent):
             value = mixed[t * SUB : (t + 1) * SUB, :]
@@ -472,10 +483,12 @@
     h, z = zero, zero
     for d in range(n):
         back = n - 1 - d
-        carry_send[d, 0:SUB, :] = h
-        carry_send[back, SUB : 2 * SUB, :] = z
-        h = whole * h + edge_recv[d, 0:SUB, :]
-        z = whole * z + edge_recv[back, SUB : 2 * SUB, :]
+        carry_hold[d, 0:SUB, :] = h
+        carry_hold[back, SUB : 2 * SUB, :] = z
+        h = whole * h + edge_recv[d].astype(f32)[0:SUB]
+        z = whole * z + edge_recv[back].astype(f32)[SUB : 2 * SUB]
+    for d in range(n):
+        carry_send[d] = carry_hold[d].astype(jnp.bfloat16)
     for peer in peers:
         send(2, peer, carry_send.at[peer], carry_recv.at[me])
     carry_recv[me] = carry_send[me]
@@ -501,14 +514,17 @@
         zeros = tuple(zero for _ in group)
         z, w = lax.fori_loop(0, tokens // UN, bwd_step, (zeros,) * 2)
         for p, m in enumerate(group):
-            acc_send[m, SUB : 2 * SUB, :] = w[p]
-
+            acc_hold[m, SUB : 2 * SUB, :] = w[p]
+
+    for m in range(modes):
+        acc_send[m] = acc_hold[m].astype(jnp.bfloat16)
     for peer in peers:
         send(3, peer, acc_send.at[peer], acc_recv.at[me])
     acc_recv[me] = acc_send[me]
 
     arrived(2, carry_recv.at[others])
     gains = per_mode(gain)
+    carried = [carry_recv[m].astype(f32) for m in range(modes)]
 
     def fwd_two(i, c):
         c = list(c)
@@ -520,7 +536,7 @@
             cots[0, slab(t), :] = streams[3, slab(t + HALO), :] * total
         return tuple(c)
 
-    start = tuple(gains[m] * carry_recv[m, 0:SUB, :] for m in range(modes))
+    start = tuple(gains[m] * carried[m][0:SUB] for m in range(modes))
     lax.fori_loop(0, extent // 2, fwd_two, start)
 
     def store_back(t, total):
@@ -536,13 +552,13 @@
             store_back(t, conv_back[slab(t), :] + tree(c))
         return tuple(c)
 
-    start = tuple(gains[m] * carry_recv[m, SUB : 2 * SUB, :] for m in range(modes))
+    start = tuple(gains[m] * carried[m][SUB : 2 * SUB] for m in range(modes))
     lax.fori_loop(0, tokens // 2, bwd_two, start)
 
     ahead = [zero] * HALO
     for m in range(modes):
         grow = jnp.exp(rate[m * SUB : (m + 1) * SUB, :])
-        z = carry_recv[m, SUB : 2 * SUB, :]
+        z = carry_recv[m].astype(f32)[SUB : 2 * SUB]
         for h in range(HALO):
             ahead[h] = ahead[h] + gains[m] * z
             z = grow * (z - gmixed[(tokens + h) * SUB : (tokens + h + 1) * SUB, :])
@@ -561,10 +577,10 @@
         return tuple(accs)
 
     accs = lax.fori_loop(0, tokens // 2, short_step, (zero,) * rows_all)
-    for row in range(2 * owners):
-        short_send[row // 2, (row % 2) * SUB : (row % 2 + 1) * SUB, :] = (
-            accs[row] if row < rows_all else zero
-        )
+    accs = list(accs) + [zero] * (2 * owners - rows_all)
+    for o in range(owners):
+        both = jnp.concatenate(accs[2 * o : 2 * o + 2], axis=0)
+        short_send[o] = both.astype(jnp.bfloat16)
     for peer in peers:
 
         @pl.when(peer < owners)
@@ -578,12 +594,13 @@
     arrived(3, acc_recv.at[others])
     hy, acc_x, acc_y = zero, zero, zero
     for d in range(n):
-        h = carry_send[d, 0:SUB, :]
-        z0 = my_decay * edge_recv[d, SUB : 2 * SUB, :]
-        z1 = my_decay * acc_recv[d, SUB : 2 * SUB, :]
-        acc_x = acc_x + (acc_recv[d, 2 * SUB : 3 * SUB, :] + h * z0)
-        acc_y = acc_y + (acc_recv[d, 3 * SUB : 4 * SUB, :] + h * z1 + hy * z0)
-        hy = whole * (hy + float(tokens) * h) + acc_recv[d, 0:SUB, :]
+        h = carry_hold[d, 0:SUB, :]
+        terms = acc_recv[d].astype(f32)
+        z0 = my_decay * edge_recv[d].astype(f32)[SUB : 2 * SUB]
+        z1 = my_decay * terms[SUB : 2 * SUB]
+        acc_x = acc_x + (terms[2 * SUB : 3 * SUB] + h * z0)
+        acc_y = acc_y + (terms[3 * SUB : 4 * SUB] + h * z1 + hy * z0)
+        hy = whole * (hy + float(tokens) * h) + terms[0:SUB]
     grad_res = acc_x * jnp.sqrt(2.0 * my_rate) * scale
     grad_log = my_gain * (0.5 * acc_x - my_rate * acc_y) * scale
     for b in range(SUB):
@@ -605,19 +622,29 @@
     @pl.when(me < owners)
     def _():
         arrived(5, short_recv.at[others])
-        total = short_recv[0]
+        total = short_recv[0].astype(f32)
         for d in range(1, n):
-            total = total + short_recv[d]
+            total = total + short_recv[d].astype(f32)
         total_send[...] = total * scale
         for peer in peers:
             send(6, peer, total_send, total_recv.at[me])
         total_recv[me] = total_send[...]
 
-    for s, ref in enumerate((out_ref, gq_ref, gk_ref, gv_ref)):
+    stores = []
+    outs = (out_ref, gq_ref, gk_ref, gv_ref)
+    for first in (0, 2):
         for b in range(SUB):
             rows = pl.ds(b, tokens, stride=SUB)
-            block = hats[s - 1, rows, :] if s else prod[rows, :]
-            ref[b * LANE : (b + 1) * LANE, :] = block.T.astype(jnp.bfloat16)
+            one = hats[first - 1, rows, :] if first else prod[rows, :]
+            block = jnp.concatenate([one, hats[first, rows, :]], axis=0)
+            block = turned(block.astype(jnp.bfloat16)).astype(jnp.bfloat16)
+            for half in range(2):
+                results[first + half, b * LANE : (b + 1) * LANE, :] = block[
+                    :, half * LANE : (half + 1) * LANE
+                ]
+        for s in (first, first + 1):
+            stores.append(pltpu.make_async_copy(results.at[s], outs[s], store_sem.at[s]))
+            stores[-1].start()
 
     arrived(4, modal_recv.at[others])
     odd_owner = lax.rem(me, 2) == 1
@@ -630,7 +657,7 @@
     def _():
         arrived(6, total_recv.at[pl.ds(0, owners - 1)])
         sent(5, short_recv.at[pl.ds(0, owners - 1)])
-        sent(6, short_recv.at[others])
+        sent(6, carry_hold.at[others])
 
     @pl.when(me >= owners)
     def _():
@@ -646,6 +673,8 @@
                     row // 2, at : at + 1, :
                 ]
 
+    for store in stores:
+        store.wait()
     sent(0, params.at[others])
     sent(1, edge_recv.at[others])
     sent(2, carry_recv.at[others])
@@ -653,16 +682,22 @@
     sent(4, modal_recv.at[others])
 
 
-def hand_over(*refs):
-    sems = refs[-1]
-    count = (len(refs) - 1) // 2
-    copies = [
-        pltpu.make_async_copy(refs[i], refs[count + i], sems.at[i]) for i in range(count)
+def hand_over(count, *refs):
+    sources, targets, held = refs[:count], refs[count : 2 * count], refs[2 * count : -2]
+    load_sem, store_sem = refs[-2:]
+    loads = [
+        pltpu.make_async_copy(sources[i], held[i], load_sem.at[i]) for i in range(count)
     ]
-    for copy in copies:
-        copy.start()
-    for copy in copies:
-        copy.wait()
+    stores = [
+        pltpu.make_async_copy(held[i], targets[i], store_sem.at[i]) for i in range(count)
+    ]
+    for load in loads:
+        load.start()
+    for load, store in zip(loads, stores):
+        load.wait()
+        store.start()
+    for store in stores:
+        store.wait()
 
 
 def local(query_in, key_in, value_in, short_weight, residue, log_rate, grad_out):
@@ -683,6 +718,8 @@
     hbm = pl.BlockSpec(memory_space=pltpu.MemorySpace.HBM)
     pair = pltpu.VMEM((n, 2 * SUB, LANE), f32)
     quad = pltpu.VMEM((n, 4 * SUB, LANE), f32)
+    half_pair = pltpu.VMEM((n, 2 * SUB, LANE), jnp.bfloat16)
+    half_quad = pltpu.VMEM((n, 4 * SUB, LANE), jnp.bfloat16)
     flat = pltpu.VMEM((rows, LANE), f32)
     triple = pltpu.VMEM((3, rows, LANE), f32)
     small = pltpu.VMEM((modes * SUB, LANE), f32)
@@ -695,21 +732,24 @@
             jax.ShapeDtypeStruct(short_weight.shape, f32), modal, modal,
         ),
         in_specs=[hbm] * 4 + [vmem] * 2,
-        out_specs=(vmem,) * 7,
+        out_specs=(hbm,) * 4 + (vmem,) * 3,
         scratch_shapes=[
+            pltpu.VMEM((4, width, tokens), jnp.bfloat16),
             pltpu.VMEM((4, width, tokens), jnp.bfloat16),
             pltpu.VMEM((4, rows + HALO * SUB, LANE), f32),
             triple, flat, flat, flat, flat, flat, triple,
             pltpu.VMEM((3 * TAPS * SUB, LANE), f32),
             pltpu.VMEM((n, modes, LANE), f32),
             small, small, small,
-            pair, pair, quad, quad, pair, pair,
+            half_pair, half_pair, quad, half_quad, half_quad,
+            pair, half_pair, half_pair,
             pltpu.VMEM((SUB, 2, LANE), f32),
             pltpu.VMEM((n, 2, LANE), f32),
-            pltpu.VMEM((owners, 2 * SUB, LANE), f32),
-            pair,
+            pltpu.VMEM((owners, 2 * SUB, LANE), jnp.bfloat16),
+            half_pair,
             pltpu.VMEM((2 * SUB, LANE), f32),
             pltpu.VMEM((owners, 2 * SUB, LANE), f32),
+            pltpu.SemaphoreType.DMA((4,)),
             pltpu.SemaphoreType.DMA((4,)),
             pltpu.SemaphoreType.DMA((7,)),
             pltpu.SemaphoreType.DMA((7,)),
@@ -722,11 +762,12 @@
     )(query_in, key_in, value_in, grad_out, short_weight, param)
     count = len(results)
     results = pl.pallas_call(
-        hand_over,
+        functools.partial(hand_over, count),
         out_shape=[jax.ShapeDtypeStruct(r.shape, r.dtype) for r in results],
         in_specs=[hbm] * count,
         out_specs=[hbm] * count,
-        scratch_shapes=[pltpu.SemaphoreType.DMA((count,))],
+        scratch_shapes=[pltpu.VMEM(r.shape, r.dtype) for r in results]
+        + [pltpu.SemaphoreType.DMA((count,))] * 2,
         compiler_params=pltpu.CompilerParams(vmem_limit_bytes=60 * 2**20),
     )(*results)
     return (*results[:5], results[5].T, results[6].T)

time: 78.7 us -> 42.3 us (0.54)
  Pallas kernels: 76.4 us -> 40 us
    pallas_call x1, Pallas kernels: 36.4 us -> 2.06 us  [local(): pl.pallas_call(functools.partial(hand_over, count), out_shape=[jax.ShapeD...]
    pallas_call x1, Pallas kernels: 40 us -> 37.9 us  [local(): pl.pallas_call(functools.partial(layer_kernel, n, modes, tokens, scale),...]
where the time goes in v2:
time: 42.3 us; the launch traced here: 42 us
  Pallas kernels  40 us (95%)
  other arithmetic  1.39 us (3%)
  between operations  0.64 us (2%)
    pallas_call x1, Pallas kernels, local(): pl.pallas_call(functools.partial(layer_kernel, n, modes, tokens, scale),...  37.9 us
    pallas_call x1, Pallas kernels, local(): pl.pallas_call(functools.partial(hand_over, count), out_shape=[jax.ShapeD...  2.06 us
    concatenate x1, other arithmetic, local(): param = jnp.concatenate([log_rate.T, residue.T], axis=1)  1.39 us

profile of v2, /device:TPU:0, one launch (start us, length us, event | category | flops | bytes accessed | tf_op | source)
XLA Modules:
  0.0 42.0 jit_solution(15006227205090043763)
XLA Ops:
  0.6 1.4 %pad_maximum_fusion.param_ref = f32[16,128]{1,0:T(8,128)} fusion(f32[16,64]{1,0:T(8,128)} %bitcast.4, f32[16,64]{1,0:T(8,128)} %bitcast.5), kind=kLoop, calls=%fused_computation | loop fusion | flops 2048 | bytes 16384 | tf_op jit(solution)/shard_map/concatenate | solution.py:716
  2.0 37.9 %shard_map.126 = (bf16[1024,128]{1,0:T(8,128)(2,1)}, bf16[1024,128]{1,0:T(8,128)(2,1)}, bf16[1024,128]{1,0:T(8,128)(2,1)}, bf16[1024,128]{1,0:T(8,128)(2,1)}, f3...) custom-call(bf16[1024,128]{1,0:T(8,128)(2,1)} %query_ref.1, bf16[1024,128]{1,0:T(8,128)(2,1)} %key_ref.1, ...), custom_call_target="tpu_custom_call" | custom-call | tf_op jit(solution)/shard_map/pallas_call | solution.py:728
  40.0 2.1 %shard_map.127 = (bf16[1024,128]{1,0:T(8,128)(2,1)}, bf16[1024,128]{1,0:T(8,128)(2,1)}, bf16[1024,128]{1,0:T(8,128)(2,1)}, bf16[1024,128]{1,0:T(8,128)(2,1)}, f3...) custom-call(bf16[1024,128]{1,0:T(8,128)(2,1)} %get-tuple-element.21.refs_0_, ...), custom_call_target="tpu_custom_call" | custom-call | tf_op jit(solution)/shard_map/pallas_call | solution.py:764

commit v3 on v2

--- a/solution.py
+++ b/solution.py
@@ -244,9 +244,9 @@
 
 def layer_kernel(
     n, modes, tokens, scale,
-    query_ref, key_ref, value_ref, grad_ref, weight_ref, param_ref,
+    query_ref, key_ref, value_ref, grad_ref, weight_ref, rate_ref, residue_ref,
     out_ref, gq_ref, gk_ref, gv_ref, short_ref, res_ref, log_ref,
-    inputs, results, streams, hats, mixed, gmixed, conv, conv_back, prod, cots,
+    inputs, results, tails, heads, tails_in, heads_in, param_ref, streams, hats, mixed, gmixed, conv, conv_back, prod, cots,
     weights, params, decay, gain, rate,
     edge_send, edge_recv, acc_hold, acc_send, acc_recv,
     carry_hold, carry_send, carry_recv, modal_send, modal_recv, short_send, short_recv, total_send, total_recv,
@@ -270,12 +270,17 @@
     def per_mode(ref):
         return [ref[m * SUB : (m + 1) * SUB, :] for m in range(modes)]
 
-    loads = [
-        pltpu.make_async_copy(ref, inputs.at[s], load_sem.at[s])
-        for s, ref in enumerate((query_ref, key_ref, value_ref, grad_ref))
-    ]
-    for load in loads:
-        load.start()
+    half_width = SUB * LANE // 2
+    loads = []
+    for s, ref in enumerate((query_ref, key_ref, value_ref, grad_ref)):
+        for half in range(2):
+            part = pl.ds(half * half_width, half_width)
+            loads.append(
+                pltpu.make_async_copy(
+                    ref.at[part], inputs.at[s, part], load_sem.at[2 * s + half]
+                )
+            )
+            loads[-1].start()
 
     barrier = pltpu.get_barrier_semaphore()
     peers = [lax.rem(me + k, n) for k in range(1, n)]
@@ -301,6 +306,7 @@
         pltpu.make_async_copy(like, like, recv_sem.at[phase]).wait()
 
     others = pl.ds(0, n - 1)
+    param_ref[...] = jnp.concatenate([rate_ref[...], residue_ref[...]], axis=1)
 
     for s in range(3):
         for b in range(SUB):
@@ -319,8 +325,9 @@
         )
 
     for s in range(4):
-        loads[s].wait()
         for b in range(0, SUB, 2):
+            if b % (SUB // 2) == 0:
+                loads[2 * s + b // (SUB // 2)].wait()
             block = turned(inputs[s, b * LANE : (b + 2) * LANE, :])
             for half in range(2):
                 streams[s, pl.ds(HALO * SUB + b + half, tokens, stride=SUB), :] = block[
@@ -335,21 +342,25 @@
     edge = HALO * SUB
     last = tokens * SUB
     to_right = lambda: pltpu.make_async_remote_copy(
-        src_ref=streams.at[pl.ds(0, 3), pl.ds(last, edge)],
-        dst_ref=streams.at[pl.ds(0, 3), pl.ds(0, edge)],
+        src_ref=tails,
+        dst_ref=tails_in,
         send_sem=halo_send.at[0],
         recv_sem=halo_recv.at[0],
         device_id={"seq": lax.rem(me + 1, n)},
         device_id_type=MESH,
     )
     to_left = lambda: pltpu.make_async_remote_copy(
-        src_ref=streams.at[:, pl.ds(edge, edge)],
-        dst_ref=streams.at[:, pl.ds(edge + last, edge)],
+        src_ref=heads,
+        dst_ref=heads_in,
         send_sem=halo_send.at[1],
         recv_sem=halo_recv.at[1],
         device_id={"seq": lax.rem(me + n - 1, n)},
         device_id_type=MESH,
     )
+    for s in range(3):
+        tails[s] = streams[s, last : last + edge, :].astype(jnp.bfloat16)
+    for s in range(4):
+        heads[s] = streams[s, edge : 2 * edge, :].astype(jnp.bfloat16)
 
     @pl.when(me < n - 1)
     def _():
@@ -358,14 +369,6 @@
     @pl.when(me > 0)
     def _():
         to_left().start()
-
-    @pl.when(me == 0)
-    def _():
-        streams[0:3, 0:edge, :] = jnp.zeros((3, edge, LANE), f32)
-
-    @pl.when(me == n - 1)
-    def _():
-        streams[:, edge + last : 2 * edge + last, :] = jnp.zeros((4, edge, LANE), f32)
 
     taps = [
         [weights[(s * TAPS + j) * SUB : (s * TAPS + j + 1) * SUB, :] for j in range(TAPS)]
@@ -392,19 +395,6 @@
         lax.fori_loop(0, (hi - lo) // unroll, step, 0)
 
     token_loop(HALO, tokens, 2, filter_token)
-
-    @pl.when(me > 0)
-    def _():
-        to_left().wait_send()
-        to_right().wait_recv()
-
-    @pl.when(me < n - 1)
-    def _():
-        to_right().wait_send()
-        to_left().wait_recv()
-
-    token_loop(0, HALO, 2, filter_token)
-    token_loop(tokens, extent, 2, filter_token)
 
     arrived(0, params.at[others])
     low_half = lax.broadcasted_iota(jnp.int32, (SUB, LANE), 1) < LANE // 2
@@ -423,16 +413,50 @@
 
     def edge_step(i, carry):
         x, z = [list(c) for c in carry]
-        for u in range(UN):
-            t = i * UN + u
-            value = mixed[slab(t), :]
+        for u in range(2):
+            t = i * 2 + u
+            value = mixed[slab(t + HALO), :]
             cot = gmixed[slab(tokens - 1 - t), :]
             for m in range(modes):
                 x[m] = decays[m] * x[m] + value
                 z[m] = decays[m] * z[m] + cot
         return tuple(x), tuple(z)
 
-    x, z = lax.fori_loop(0, tokens // UN, edge_step, ((zero,) * modes,) * 2)
+    inner = tokens - HALO
+    x, z = lax.fori_loop(0, inner // 2, edge_step, ((zero,) * modes,) * 2)
+    @pl.when(me > 0)
+    def _():
+        to_left().wait_send()
+        to_right().wait_recv()
+        for s in range(3):
+            streams[s, 0:edge, :] = tails_in[s].astype(f32)
+
+    @pl.when(me == 0)
+    def _():
+        streams[0:3, 0:edge, :] = jnp.zeros((3, edge, LANE), f32)
+
+    @pl.when(me < n - 1)
+    def _():
+        to_right().wait_send()
+        to_left().wait_recv()
+        for s in range(4):
+            streams[s, edge + last : 2 * edge + last, :] = heads_in[s].astype(f32)
+
+    @pl.when(me == n - 1)
+    def _():
+        streams[:, edge + last : 2 * edge + last, :] = jnp.zeros((4, edge, LANE), f32)
+
+    token_loop(0, HALO, 2, filter_token)
+    token_loop(tokens, extent, 2, filter_token)
+
+    x, z = list(x), list(z)
+    for m in range(modes):
+        early = zero
+        for t in range(HALO):
+            back = HALO - 1 - t
+            early = decays[m] * early + mixed[t * SUB : (t + 1) * SUB, :]
+            z[m] = decays[m] * z[m] + gmixed[back * SUB : (back + 1) * SUB, :]
+        x[m] = x[m] + jnp.exp(-float(inner) * rate[m * SUB : (m + 1) * SUB, :]) * early
     for m in range(modes):
         edge_send[m] = jnp.concatenate([x[m], z[m]], axis=0).astype(jnp.bfloat16)
     for peer in peers:
@@ -625,7 +649,7 @@
         total = short_recv[0].astype(f32)
         for d in range(1, n):
             total = total + short_recv[d].astype(f32)
-        total_send[...] = total * scale
+        total_send[...] = (total * scale).astype(jnp.bfloat16)
         for peer in peers:
             send(6, peer, total_send, total_recv.at[me])
         total_recv[me] = total_send[...]
@@ -657,21 +681,20 @@
     def _():
         arrived(6, total_recv.at[pl.ds(0, owners - 1)])
         sent(5, short_recv.at[pl.ds(0, owners - 1)])
-        sent(6, carry_hold.at[others])
+        sent(6, short_recv.at[others])
 
     @pl.when(me >= owners)
     def _():
         arrived(6, total_recv)
         sent(5, short_recv.at[pl.ds(0, owners)])
 
-    for s in range(3):
-        for b in range(SUB):
-            for j in range(TAPS):
-                row = s * TAPS + j
+    for o in range(owners):
+        both = total_recv[o].astype(f32)
+        for row in range(2 * o, min(2 * o + 2, rows_all)):
+            s, j = row // TAPS, row % TAPS
+            for b in range(SUB):
                 at = (row % 2) * SUB + b
-                short_ref[s, j : j + 1, b * LANE : (b + 1) * LANE] = total_recv[
-                    row // 2, at : at + 1, :
-                ]
+                short_ref[s, j : j + 1, b * LANE : (b + 1) * LANE] = both[at : at + 1]
 
     for store in stores:
         store.wait()
@@ -713,13 +736,14 @@
     f32 = jnp.float32
     rows = (tokens + HALO) * SUB
     owners = (3 * TAPS + 1) // 2
-    param = jnp.concatenate([log_rate.T, residue.T], axis=1)
     vmem = pl.BlockSpec(memory_space=pltpu.VMEM)
     hbm = pl.BlockSpec(memory_space=pltpu.MemorySpace.HBM)
     pair = pltpu.VMEM((n, 2 * SUB, LANE), f32)
     quad = pltpu.VMEM((n, 4 * SUB, LANE), f32)
     half_pair = pltpu.VMEM((n, 2 * SUB, LANE), jnp.bfloat16)
     half_quad = pltpu.VMEM((n, 4 * SUB, LANE), jnp.bfloat16)
+    tail = pltpu.VMEM((3, HALO * SUB, LANE), jnp.bfloat16)
+    head = pltpu.VMEM((4, HALO * SUB, LANE), jnp.bfloat16)
     flat = pltpu.VMEM((rows, LANE), f32)
     triple = pltpu.VMEM((3, rows, LANE), f32)
     small = pltpu.VMEM((modes * SUB, LANE), f32)
@@ -731,11 +755,13 @@
             shape, shape, shape, shape,
             jax.ShapeDtypeStruct(short_weight.shape, f32), modal, modal,
         ),
-        in_specs=[hbm] * 4 + [vmem] * 2,
+        in_specs=[hbm] * 4 + [vmem] * 3,
         out_specs=(hbm,) * 4 + (vmem,) * 3,
         scratch_shapes=[
             pltpu.VMEM((4, width, tokens), jnp.bfloat16),
             pltpu.VMEM((4, width, tokens), jnp.bfloat16),
+            tail, head, tail, head,
+            pltpu.VMEM((modes, LANE), f32),
             pltpu.VMEM((4, rows + HALO * SUB, LANE), f32),
             triple, flat, flat, flat, flat, flat, triple,
             pltpu.VMEM((3 * TAPS * SUB, LANE), f32),
@@ -747,9 +773,9 @@
             pltpu.VMEM((n, 2, LANE), f32),
             pltpu.VMEM((owners, 2 * SUB, LANE), jnp.bfloat16),
             half_pair,
-            pltpu.VMEM((2 * SUB, LANE), f32),
-            pltpu.VMEM((owners, 2 * SUB, LANE), f32),
-            pltpu.SemaphoreType.DMA((4,)),
+            pltpu.VMEM((2 * SUB, LANE), jnp.bfloat16),
+            pltpu.VMEM((owners, 2 * SUB, LANE), jnp.bfloat16),
+            pltpu.SemaphoreType.DMA((8,)),
             pltpu.SemaphoreType.DMA((4,)),
             pltpu.SemaphoreType.DMA((7,)),
             pltpu.SemaphoreType.DMA((7,)),
@@ -759,7 +785,7 @@
         compiler_params=pltpu.CompilerParams(
             collective_id=0, has_side_effects=True, vmem_limit_bytes=56 * 2**20
         ),
-    )(query_in, key_in, value_in, grad_out, short_weight, param)
+    )(query_in, key_in, value_in, grad_out, short_weight, log_rate.T, residue.T)
     count = len(results)
     results = pl.pallas_call(
         functools.partial(hand_over, count),

time: 42.3 us -> 39.7 us (0.939)
  other arithmetic: 1.39 us -> 0 us
  Pallas kernels: 40 us -> 38.8 us
    concatenate x1 -> x0, other arithmetic: 1.39 us -> none  [local(): param = jnp.concatenate([log_rate.T, residue.T], axis=1)]
    pallas_call x1, Pallas kernels: 37.9 us -> 36.8 us  [local(): pl.pallas_call(functools.partial(layer_kernel, n, modes, tokens, scale),...]
where the time goes in v3:
time: 39.7 us; the launch traced here: 39.5 us
  Pallas kernels  38.8 us (98%)
  between operations  0.64 us (2%)
    pallas_call x1, Pallas kernels, local(): pl.pallas_call(functools.partial(layer_kernel, n, modes, tokens, scale),...  36.8 us
    pallas_call x1, Pallas kernels, local(): pl.pallas_call(functools.partial(hand_over, count), out_shape=[jax.ShapeD...  2.06 us

profile of v3, /device:TPU:0, one launch (start us, length us, event | category | flops | bytes accessed | tf_op | source)
XLA Modules:
  0.0 39.5 jit_solution(2741599308569741927)
XLA Ops:
  0.6 36.8 %shard_map.126 = (bf16[1024,128]{1,0:T(8,128)(2,1)}, bf16[1024,128]{1,0:T(8,128)(2,1)}, bf16[1024,128]{1,0:T(8,128)(2,1)}, bf16[1024,128]{1,0:T(8,128)(2,1)}, f3...) custom-call(bf16[1024,128]{1,0:T(8,128)(2,1)} %query_ref.1, bf16[1024,128]{1,0:T(8,128)(2,1)} %key_ref.1, ...), custom_call_target="tpu_custom_call" | custom-call | tf_op jit(solution)/shard_map/pallas_call | solution.py:752
  37.4 2.1 %shard_map.127 = (bf16[1024,128]{1,0:T(8,128)(2,1)}, bf16[1024,128]{1,0:T(8,128)(2,1)}, bf16[1024,128]{1,0:T(8,128)(2,1)}, bf16[1024,128]{1,0:T(8,128)(2,1)}, f3...) custom-call(bf16[1024,128]{1,0:T(8,128)(2,1)} %get-tuple-element.21.refs_0_, ...), custom_call_target="tpu_custom_call" | custom-call | tf_op jit(solution)/shard_map/pallas_call | solution.py:790

commit v4 on v3

--- a/solution.py
+++ b/solution.py
@@ -249,7 +249,7 @@
     inputs, results, tails, heads, tails_in, heads_in, param_ref, streams, hats, mixed, gmixed, conv, conv_back, prod, cots,
     weights, params, decay, gain, rate,
     edge_send, edge_recv, acc_hold, acc_send, acc_recv,
-    carry_hold, carry_send, carry_recv, modal_send, modal_recv, short_send, short_recv, total_send, total_recv,
+    carry_hold, carry_send, carry_recv, modal_send, modal_recv, short_send, short_recv, total_send, total_recv, totals,
     load_sem, store_sem, send_sem, recv_sem, halo_send, halo_recv,
 ):
     me = lax.axis_index("seq")
@@ -283,7 +283,8 @@
             loads[-1].start()
 
     barrier = pltpu.get_barrier_semaphore()
-    peers = [lax.rem(me + k, n) for k in range(1, n)]
+    offsets = sorted(range(1, n), key=lambda k: abs(2 * k - n))
+    peers = [lax.rem(me + k, n) for k in offsets]
     for peer in peers:
         pl.semaphore_signal(
             barrier, inc=1, device_id={"seq": peer}, device_id_type=MESH
@@ -324,6 +325,7 @@
             eye, block, (((1,), (1,)), ((), ())), preferred_element_type=f32
         )
 
+    own_rows = pl.ds(pl.multiple_of(me * modes, modes), modes)
     for s in range(4):
         for b in range(0, SUB, 2):
             if b % (SUB // 2) == 0:
@@ -336,8 +338,8 @@
         if s == 1:
             pl.semaphore_wait(barrier, n - 1)
             for peer in peers:
-                send(0, peer, param_ref, params.at[me])
-            params[me] = param_ref[...]
+                send(0, peer, param_ref, params.at[own_rows])
+            params[own_rows, :] = param_ref[...]
 
     edge = HALO * SUB
     last = tokens * SUB
@@ -396,11 +398,11 @@
 
     token_loop(HALO, tokens, 2, filter_token)
 
-    arrived(0, params.at[others])
+    arrived(0, params.at[pl.ds(0, (n - 1) * modes)])
     low_half = lax.broadcasted_iota(jnp.int32, (SUB, LANE), 1) < LANE // 2
     for m in range(modes):
-        even = jnp.concatenate([params[2 * b, m : m + 1, :] for b in range(SUB)], axis=0)
-        odd = jnp.concatenate([params[2 * b + 1, m : m + 1, :] for b in range(SUB)], axis=0)
+        even = params[pl.ds(m, SUB, stride=2 * modes), :]
+        odd = params[pl.ds(modes + m, SUB, stride=2 * modes), :]
         log_rate = jnp.where(low_half, even, pltpu.roll(odd, LANE // 2, 1))
         residue = jnp.where(low_half, pltpu.roll(even, LANE // 2, 1), odd)
         r = jnp.exp(log_rate)
@@ -689,16 +691,16 @@
         sent(5, short_recv.at[pl.ds(0, owners)])
 
     for o in range(owners):
-        both = total_recv[o].astype(f32)
-        for row in range(2 * o, min(2 * o + 2, rows_all)):
-            s, j = row // TAPS, row % TAPS
-            for b in range(SUB):
-                at = (row % 2) * SUB + b
-                short_ref[s, j : j + 1, b * LANE : (b + 1) * LANE] = both[at : at + 1]
+        totals[2 * o * SUB : 2 * (o + 1) * SUB, :] = total_recv[o].astype(f32)
+    for s in range(3):
+        for b in range(SUB):
+            short_ref[s, :, b * LANE : (b + 1) * LANE] = totals[
+                pl.ds(s * TAPS * SUB + b, TAPS, stride=SUB), :
+            ]
 
     for store in stores:
         store.wait()
-    sent(0, params.at[others])
+    sent(0, params.at[pl.ds(0, (n - 1) * modes)])
     sent(1, edge_recv.at[others])
     sent(2, carry_recv.at[others])
     sent(3, acc_recv.at[others])
@@ -708,12 +710,17 @@
 def hand_over(count, *refs):
     sources, targets, held = refs[:count], refs[count : 2 * count], refs[2 * count : -2]
     load_sem, store_sem = refs[-2:]
-    loads = [
-        pltpu.make_async_copy(sources[i], held[i], load_sem.at[i]) for i in range(count)
-    ]
-    stores = [
-        pltpu.make_async_copy(held[i], targets[i], store_sem.at[i]) for i in range(count)
-    ]
+    pieces = []
+    for i in range(count):
+        lead = sources[i].shape[0]
+        cuts = 4 if lead % 64 == 0 else 1
+        for c in range(cuts):
+            pieces.append((i, pl.ds(c * (lead // cuts), lead // cuts)))
+    loads, stores = [], []
+    for at, (i, part) in enumerate(pieces):
+        middle = held[i].at[part]
+        loads.append(pltpu.make_async_copy(sources[i].at[part], middle, load_sem.at[at]))
+        stores.append(pltpu.make_async_copy(middle, targets[i].at[part], store_sem.at[at]))
     for load in loads:
         load.start()
     for load, store in zip(loads, stores):
@@ -765,7 +772,7 @@
             pltpu.VMEM((4, rows + HALO * SUB, LANE), f32),
             triple, flat, flat, flat, flat, flat, triple,
             pltpu.VMEM((3 * TAPS * SUB, LANE), f32),
-            pltpu.VMEM((n, modes, LANE), f32),
+            pltpu.VMEM((n * modes, LANE), f32),
             small, small, small,
             half_pair, half_pair, quad, half_quad, half_quad,
             pair, half_pair, half_pair,
@@ -775,6 +782,7 @@
             half_pair,
             pltpu.VMEM((2 * SUB, LANE), jnp.bfloat16),
             pltpu.VMEM((owners, 2 * SUB, LANE), jnp.bfloat16),
+            pltpu.VMEM((owners * 2 * SUB, LANE), f32),
             pltpu.SemaphoreType.DMA((8,)),
             pltpu.SemaphoreType.DMA((4,)),
             pltpu.SemaphoreType.DMA((7,)),
@@ -793,7 +801,7 @@
         in_specs=[hbm] * count,
         out_specs=[hbm] * count,
         scratch_shapes=[pltpu.VMEM(r.shape, r.dtype) for r in results]
-        + [pltpu.SemaphoreType.DMA((count,))] * 2,
+        + [pltpu.SemaphoreType.DMA((4 * count,))] * 2,
         compiler_params=pltpu.CompilerParams(vmem_limit_bytes=60 * 2**20),
     )(*results)
     return (*results[:5], results[5].T, results[6].T)

time: 39.7 us -> 40.4 us (1.018)
  Pallas kernels: 38.8 us -> 39.5 us
where the time goes in v4:
time: 40.4 us; the launch traced here: 40.2 us
  Pallas kernels  39.5 us (98%)
  between operations  0.64 us (2%)
    pallas_call x1, Pallas kernels, local(): pl.pallas_call(functools.partial(layer_kernel, n, modes, tokens, scale),...  37.1 us
    pallas_call x1, Pallas kernels, local(): pl.pallas_call(functools.partial(hand_over, count), out_shape=[jax.ShapeD...  2.46 us

profile of v4, /device:TPU:0, one launch (start us, length us, event | category | flops | bytes accessed | tf_op | source)
XLA Modules:
  0.0 40.2 jit_solution(16299856590467623639)
XLA Ops:
  0.6 37.1 %shard_map.126 = (bf16[1024,128]{1,0:T(8,128)(2,1)}, bf16[1024,128]{1,0:T(8,128)(2,1)}, bf16[1024,128]{1,0:T(8,128)(2,1)}, bf16[1024,128]{1,0:T(8,128)(2,1)}, f3...) custom-call(bf16[1024,128]{1,0:T(8,128)(2,1)} %query_ref.1, bf16[1024,128]{1,0:T(8,128)(2,1)} %key_ref.1, ...), custom_call_target="tpu_custom_call" | custom-call | tf_op jit(solution)/shard_map/pallas_call | solution.py:759
  37.7 2.5 %shard_map.127 = (bf16[1024,128]{1,0:T(8,128)(2,1)}, bf16[1024,128]{1,0:T(8,128)(2,1)}, bf16[1024,128]{1,0:T(8,128)(2,1)}, bf16[1024,128]{1,0:T(8,128)(2,1)}, f3...) custom-call(bf16[1024,128]{1,0:T(8,128)(2,1)} %get-tuple-element.21.refs_0_, ...), custom_call_target="tpu_custom_call" | custom-call | tf_op jit(solution)/shard_map/pallas_call | solution.py:798

commit v5 on v4

--- a/solution.py
+++ b/solution.py
@@ -270,6 +270,13 @@
     def per_mode(ref):
         return [ref[m * SUB : (m + 1) * SUB, :] for m in range(modes)]
 
+    barrier = pltpu.get_barrier_semaphore()
+    peers = [lax.rem(me + k, n) for k in range(1, n)]
+    for peer in peers:
+        pl.semaphore_signal(
+            barrier, inc=1, device_id={"seq": peer}, device_id_type=MESH
+        )
+
     half_width = SUB * LANE // 2
     loads = []
     for s, ref in enumerate((query_ref, key_ref, value_ref, grad_ref)):
@@ -281,14 +288,6 @@
                 )
             )
             loads[-1].start()
-
-    barrier = pltpu.get_barrier_semaphore()
-    offsets = sorted(range(1, n), key=lambda k: abs(2 * k - n))
-    peers = [lax.rem(me + k, n) for k in offsets]
-    for peer in peers:
-        pl.semaphore_signal(
-            barrier, inc=1, device_id={"seq": peer}, device_id_type=MESH
-        )
 
     def send(phase, peer, source, target):
         pltpu.make_async_remote_copy(
@@ -710,17 +709,12 @@
 def hand_over(count, *refs):
     sources, targets, held = refs[:count], refs[count : 2 * count], refs[2 * count : -2]
     load_sem, store_sem = refs[-2:]
-    pieces = []
-    for i in range(count):
-        lead = sources[i].shape[0]
-        cuts = 4 if lead % 64 == 0 else 1
-        for c in range(cuts):
-            pieces.append((i, pl.ds(c * (lead // cuts), lead // cuts)))
-    loads, stores = [], []
-    for at, (i, part) in enumerate(pieces):
-        middle = held[i].at[part]
-        loads.append(pltpu.make_async_copy(sources[i].at[part], middle, load_sem.at[at]))
-        stores.append(pltpu.make_async_copy(middle, targets[i].at[part], store_sem.at[at]))
+    loads = [
+        pltpu.make_async_copy(sources[i], held[i], load_sem.at[i]) for i in range(count)
+    ]
+    stores = [
+        pltpu.make_async_copy(held[i], targets[i], store_sem.at[i]) for i in range(count)
+    ]
     for load in loads:
         load.start()
     for load, store in zip(loads, stores):
@@ -801,7 +795,7 @@
         in_specs=[hbm] * count,
         out_specs=[hbm] * count,
         scratch_shapes=[pltpu.VMEM(r.shape, r.dtype) for r in results]
-        + [pltpu.SemaphoreType.DMA((4 * count,))] * 2,
+        + [pltpu.SemaphoreType.DMA((count,))] * 2,
         compiler_params=pltpu.CompilerParams(vmem_limit_bytes=60 * 2**20),
     )(*results)
     return (*results[:5], results[5].T, results[6].T)

time: 40.4 us -> 39.6 us (0.980)
  Pallas kernels: 39.5 us -> 38.8 us
where the time goes in v5:
time: 39.6 us; the launch traced here: 39.4 us
  Pallas kernels  38.8 us (98%)
  between operations  0.64 us (2%)
    pallas_call x1, Pallas kernels, local(): pl.pallas_call(functools.partial(layer_kernel, n, modes, tokens, scale),...  36.7 us
    pallas_call x1, Pallas kernels, local(): pl.pallas_call(functools.partial(hand_over, count), out_shape=[jax.ShapeD...  2.06 us

profile of v5, /device:TPU:0, one launch (start us, length us, event | category | flops | bytes accessed | tf_op | source)
XLA Modules:
  0.0 39.4 jit_solution(9875883156574913830)
XLA Ops:
  0.6 36.7 %shard_map.126 = (bf16[1024,128]{1,0:T(8,128)(2,1)}, bf16[1024,128]{1,0:T(8,128)(2,1)}, bf16[1024,128]{1,0:T(8,128)(2,1)}, bf16[1024,128]{1,0:T(8,128)(2,1)}, f3...) custom-call(bf16[1024,128]{1,0:T(8,128)(2,1)} %query_ref.1, bf16[1024,128]{1,0:T(8,128)(2,1)} %key_ref.1, ...), custom_call_target="tpu_custom_call" | custom-call | tf_op jit(solution)/shard_map/pallas_call | solution.py:753
  37.4 2.1 %shard_map.127 = (bf16[1024,128]{1,0:T(8,128)(2,1)}, bf16[1024,128]{1,0:T(8,128)(2,1)}, bf16[1024,128]{1,0:T(8,128)(2,1)}, bf16[1024,128]{1,0:T(8,128)(2,1)}, f3...) custom-call(bf16[1024,128]{1,0:T(8,128)(2,1)} %get-tuple-element.21.refs_0_, ...), custom_call_target="tpu_custom_call" | custom-call | tf_op jit(solution)/shard_map/pallas_call | solution.py:792
